TPU v7x, 32 devices: a whole 2x2x4 slice. The times are simulated.
32 devices in a mesh: batch: 16 (over z, y, x), tensor: 2 (over core).
Axes of the slice: x: 2, y: 2, z: 4, core: 2. Of those that a mesh axis runs over, the one named last changes fastest.
Arguments:
- inputs: bfloat16 [2, 8192, 768], P(None, ('batch', 'tensor')), may hold values from -6 to 6
- cotangent: bfloat16 [2, 8192, 768], P(None, ('batch', 'tensor')), may hold values from -6 to 6
- lengths: int32 [2, 16, 16], P(None, 'batch'), may hold values from 1 to 384, 512 in all within a row
- owners: int32 [256], replicated, may hold values from 0 to 15, as said below
- vectors: float32 [512, 28], P('batch'), may hold values from -4 to 4
- first_moment: float32 [512, 28], P('batch'), may hold values from -160 to 160
- second_moment: float32 [512, 28], P('batch'), may hold values from 737.28 to 2949.12
- weight_in: bfloat16 [2, 768, 3, 768], P(None, 'batch', None, 'tensor'), may hold values from -0.21875 to 0.21875
- weight_out: bfloat16 [2, 768, 768], P(None, 'tensor', 'batch'), may hold values from -0.875 to 0.875
- weight_up: bfloat16 [2, 768, 3072], P(None, 'batch', 'tensor'), may hold values from -0.21875 to 0.21875
- weight_down: bfloat16 [2, 3072, 768], P(None, 'tensor', 'batch'), may hold values from -0.109375 to 0.109375
- basis_a: bfloat16 [1024, 768], P('batch'), may hold values from -0.21875 to 0.21875
- basis_b: bfloat16 [768, 1024], P('tensor', 'batch'), may hold values from -0.1875 to 0.1875
- norm_gain: float32 [2, 2, 768], replicated, may hold values from 0.5 to 1.5
- norm_bias: float32 [2, 2, 768], replicated, may hold values from -2 to 2
Outputs:
- outputs: bfloat16 [2, 8192, 768], P(None, ('batch', 'tensor'))
- input_grads: float32 [2, 8192, 768], P(None, ('batch', 'tensor'))
- vector_grads: float32 [512, 28], P('batch')
- new_first_moment: float32 [512, 28], P('batch')
- new_second_moment: float32 [512, 28], P('batch')
- new_vectors: float32 [512, 28], P('batch')
- new_vectors_low: bfloat16 [512, 28], P('batch')
Inputs may be any that keep to these rules, and one draw needn't show every extreme that they name: Batch index b owns the pieces c with owners[c] = b; none owns more than 32 pieces and some owns exactly 32.
All inputs are finite; a program needn't handle non-finite values.
Results may differ from a plain program's by a relative error of at most 0.039.
Values may be sent and summed in bfloat16 or wider, within the bound.
A program may use at most 192 MiB of HBM per device.

v0:
```python
import jax
import jax.numpy as jnp
from jax import lax
from jax.sharding import PartitionSpec as P

D = 768
HDIM = 64
R = 1024
LAYERS = 2
STEP = 10


EPSILON = 1e-05
SCORE_SCALE = 0.125
MASKED_SCORE = -1000000000.0
LEARN_RATE = 0.3
WEIGHT_DECAY = 0.01
FIRST_BETA = 0.5
SECOND_BETA = 0.5
ADAM_EPSILON = 1e-08


def normalize(values, gain_row, offset):
    center = values - jnp.mean(values, axis=-1, keepdims=True)
    spread = jnp.mean(center * center, axis=-1, keepdims=True)
    return center * lax.rsqrt(spread + EPSILON) * gain_row + offset


def norm_back(values, gain_row, offset, upstream):
    _, pullback = jax.vjp(lambda argument: normalize(argument, gain_row, offset), values)
    return pullback(upstream)[0]


def gelu_back(before, upstream):
    _, pullback = jax.vjp(lambda argument: jax.nn.gelu(argument, approximate=False), before)
    return pullback(upstream)[0]


def product(left, right, form):
    return jnp.einsum(form, left, right, preferred_element_type=jnp.float32)


def segment_ids(doc_sizes, total_rows):
    doc_ends = jnp.cumsum(doc_sizes)
    places = jnp.arange(total_rows, dtype=jnp.int32)
    return jnp.sum((doc_ends[None, :] <= places[:, None]).astype(jnp.int32), axis=1)


def owner_tables(owners, batch_index, slot_count):
    span_count = owners.shape[0]
    span_ids = jnp.arange(span_count, dtype=jnp.int32)
    same_owner = owners[:, None] == owners[None, :]
    earlier = span_ids[None, :] < span_ids[:, None]
    owner_ranks = jnp.sum((same_owner & earlier).astype(jnp.int32), axis=1)
    slot_of = owners * slot_count + owner_ranks
    own_span = owners == batch_index
    slot_ids = jnp.arange(slot_count, dtype=jnp.int32)
    select = ((owner_ranks[None, :] == slot_ids[:, None]) & own_span[None, :]).astype(jnp.float32)
    filled = jnp.sum(select, axis=1, keepdims=True)
    return (slot_of, select, filled)


def block_scores(query_block, key_rows, ids_block, ids_all):
    scores = product(query_block, key_rows, "qhe,khe->hqk") * SCORE_SCALE
    return jnp.where((ids_block[:, None] == ids_all[None, :])[None], scores, MASKED_SCORE)


def attend(query_rows, key_rows, value_rows, ids_all):
    scores = block_scores(query_rows, key_rows, ids_all, ids_all)
    highest = jnp.max(scores, axis=-1, keepdims=True)
    exponent_values = jnp.exp(scores - highest)
    totals = jnp.sum(exponent_values, axis=-1, keepdims=True)
    chances = (exponent_values / totals).astype(jnp.bfloat16)
    outputs = product(chances, value_rows, "hqk,khe->qhe")
    logsums = [highest + jnp.log(totals)]
    return (outputs, logsums)


def attend_back(query_rows, key_rows, value_rows, ids_all, logsums, out_grad):
    total_rows = query_rows.shape[0]
    block_rows = min(512, total_rows)
    query_grads = []
    key_grad = jnp.zeros(key_rows.shape, jnp.float32)
    value_grad = jnp.zeros(value_rows.shape, jnp.float32)
    for number, block_start in enumerate(range(0, total_rows, block_rows)):
        scores = block_scores(query_rows, key_rows, ids_all, ids_all)
        chances = jnp.exp(scores - logsums[number])
        chance_grad = product(out_grad, value_rows, "qhe,khe->hqk")
        inner_sum = jnp.sum(chances * chance_grad, axis=-1, keepdims=True)
        score_grad = (chances * (chance_grad - inner_sum)).astype(jnp.bfloat16)
        query_grads.append(product(score_grad, key_rows, "hqk,khe->qhe") * SCORE_SCALE)
        key_grad = product(score_grad, query_rows, "hqk,qhe->khe") * SCORE_SCALE
        value_grad = product(chances.astype(jnp.bfloat16), out_grad, "hqk,qhe->khe")
    return (query_grads[0], key_grad, value_grad)


def layer_forward(rows_half, rows_low, trained, weights, ids_all):
    scale_q, scale_v, bias_q, bias_v = trained
    weight_in, weight_out, weight_up, weight_down, basis_a, basis_b, norm_gains, offsets = weights
    total_rows = rows_low.shape[0]
    feature_width = weight_out.shape[0]
    projected = product(rows_low, basis_a, "td,rd->tr")
    adapt_q = product((scale_q * projected).astype(jnp.bfloat16), basis_b, "tr,wr->tw")
    adapt_v = product((scale_v * projected).astype(jnp.bfloat16), basis_b, "tr,wr->tw")
    frozen_qkv = product(rows_low, weight_in, "td,dcw->tcw")
    query_rows = (
        (frozen_qkv[:, 0] + bias_q * adapt_q).astype(jnp.bfloat16).reshape(total_rows, -1, HDIM)
    )
    key_rows = frozen_qkv[:, 1].astype(jnp.bfloat16).reshape(total_rows, -1, HDIM)
    value_rows = (
        (frozen_qkv[:, 2] + bias_v * adapt_v).astype(jnp.bfloat16).reshape(total_rows, -1, HDIM)
    )
    mixed_rows, logsums = attend(query_rows, key_rows, value_rows, ids_all)
    mixed_low = mixed_rows.reshape(total_rows, feature_width).astype(jnp.bfloat16)
    first_sum = rows_half + lax.psum_scatter(
        jnp.dot(mixed_low, weight_out, preferred_element_type=jnp.float32).astype(jnp.bfloat16),
        "tensor",
        scatter_dimension=0,
        tiled=True,
    ).astype(jnp.float32)
    middle = normalize(first_sum, norm_gains[0], offsets[0])
    middle_low = lax.all_gather(middle.astype(jnp.bfloat16), "tensor", axis=0, tiled=True)
    before = jnp.dot(middle_low, weight_up, preferred_element_type=jnp.float32)
    active = jax.nn.gelu(before, approximate=False).astype(jnp.bfloat16)
    second_sum = middle + lax.psum_scatter(
        jnp.dot(active, weight_down, preferred_element_type=jnp.float32).astype(jnp.bfloat16),
        "tensor",
        scatter_dimension=0,
        tiled=True,
    ).astype(jnp.float32)
    result = normalize(second_sum, norm_gains[1], offsets[1])
    kept_values = (
        projected,
        adapt_q,
        adapt_v,
        query_rows,
        key_rows,
        value_rows,
        logsums,
        first_sum,
        before,
        second_sum,
    )
    return (result, kept_values)


def layer_backward(upstream, kept_values, trained, weights, ids_all):
    scale_q, scale_v, bias_q, bias_v = trained
    weight_in, weight_out, weight_up, weight_down, basis_a, basis_b, norm_gains, offsets = weights
    (
        projected,
        adapt_q,
        adapt_v,
        query_rows,
        key_rows,
        value_rows,
        logsums,
        first_sum,
        before,
        second_sum,
    ) = kept_values
    total_rows = query_rows.shape[0]
    feature_width = weight_out.shape[0]
    second_grad = norm_back(second_sum, norm_gains[1], offsets[1], upstream)
    feed_grad = lax.all_gather(second_grad.astype(jnp.bfloat16), "tensor", axis=0, tiled=True)
    active_grad = product(feed_grad, weight_down, "td,fd->tf")
    before_grad = gelu_back(before, active_grad).astype(jnp.bfloat16)
    middle_grad = second_grad + lax.psum_scatter(
        product(before_grad, weight_up, "tf,df->td").astype(jnp.bfloat16),
        "tensor",
        scatter_dimension=0,
        tiled=True,
    ).astype(jnp.float32)
    first_grad = norm_back(first_sum, norm_gains[0], offsets[0], middle_grad)
    branch_grad = lax.all_gather(first_grad.astype(jnp.bfloat16), "tensor", axis=0, tiled=True)
    mixed_grad = (
        product(branch_grad, weight_out, "td,wd->tw")
        .astype(jnp.bfloat16)
        .reshape(total_rows, -1, HDIM)
    )
    query_grad, key_grad, value_grad = attend_back(
        query_rows, key_rows, value_rows, ids_all, logsums, mixed_grad
    )
    query_grad = query_grad.reshape(total_rows, feature_width).astype(jnp.bfloat16)
    key_grad = key_grad.reshape(total_rows, feature_width).astype(jnp.bfloat16)
    value_grad = value_grad.reshape(total_rows, feature_width).astype(jnp.bfloat16)
    query_wide = query_grad.astype(jnp.float32)
    value_wide = value_grad.astype(jnp.float32)
    from_q = product((bias_q * query_wide).astype(jnp.bfloat16), basis_b, "tw,wr->tr")
    from_v = product((bias_v * value_wide).astype(jnp.bfloat16), basis_b, "tw,wr->tr")
    trained_grads = (
        jnp.sum(projected * from_q, axis=0),
        jnp.sum(projected * from_v, axis=0),
        jnp.sum(query_wide * adapt_q, axis=0),
        jnp.sum(value_wide * adapt_v, axis=0),
    )
    projected_grad = (scale_q * from_q + scale_v * from_v).astype(jnp.bfloat16)
    total = product(query_grad, weight_in[:, 0], "tw,dw->td")
    total = total + product(key_grad, weight_in[:, 1], "tw,dw->td")
    total = total + product(value_grad, weight_in[:, 2], "tw,dw->td")
    input_grad = first_grad + lax.psum_scatter(
        (total + jnp.dot(projected_grad, basis_a, preferred_element_type=jnp.float32)).astype(
            jnp.bfloat16
        ),
        "tensor",
        scatter_dimension=0,
        tiled=True,
    ).astype(jnp.float32)
    return (input_grad, trained_grads)


def on_device(
    inputs,
    cotangent,
    lengths,
    owners,
    vectors,
    first_moment,
    second_moment,
    weight_in,
    weight_out,
    weight_up,
    weight_down,
    basis_a,
    basis_b,
    norm_gain,
    norm_bias,
):
    tensor_count = lax.axis_size("tensor")
    tensor_index = lax.axis_index("tensor")
    batch_index = lax.axis_index("batch")
    micro_count, half_rows, _ = inputs.shape
    total_rows = half_rows * tensor_count
    feature_width = D // tensor_count
    slot_count = vectors.shape[0]
    slot_of, select, filled = owner_tables(owners, batch_index, slot_count)
    all_slots = lax.all_gather(vectors, "batch", axis=0, tiled=True)
    flat = jnp.take(all_slots, slot_of, axis=0).reshape(LAYERS, 2 * R + 2 * D)
    trained = []
    for layer_index in range(LAYERS):
        row_params = flat[layer_index]
        trained.append(
            (
                row_params[:R],
                row_params[R : 2 * R],
                lax.dynamic_slice_in_dim(
                    row_params[2 * R : 2 * R + D], tensor_index * feature_width, feature_width, 0
                ),
                lax.dynamic_slice_in_dim(
                    row_params[2 * R + D :], tensor_index * feature_width, feature_width, 0
                ),
            )
        )

    def layer_weights(fetched, layer_index):
        return (
            fetched[0][layer_index],
            fetched[1][layer_index],
            fetched[2][layer_index],
            fetched[3][layer_index],
            fetched[4],
            fetched[5],
            norm_gain[layer_index],
            norm_bias[layer_index],
        )

    grad_totals = [
        (
            jnp.zeros((R,), jnp.float32),
            jnp.zeros((R,), jnp.float32),
            jnp.zeros((feature_width,), jnp.float32),
            jnp.zeros((feature_width,), jnp.float32),
        )
        for layer_index in range(LAYERS)
    ]
    results = []
    input_grads = []
    for micro_index in range(micro_count):
        fetched = (
            lax.all_gather(weight_in, "batch", axis=1, tiled=True),
            lax.all_gather(weight_out, "batch", axis=2, tiled=True),
            lax.all_gather(weight_up, "batch", axis=1, tiled=True),
            lax.all_gather(weight_down, "batch", axis=2, tiled=True),
            lax.all_gather(basis_a, "batch", axis=0, tiled=True),
            lax.all_gather(basis_b, "batch", axis=1, tiled=True),
        )
        ids_all = segment_ids(lengths[micro_index, 0], total_rows)
        rows_half = inputs[micro_index].astype(jnp.float32)
        kept_layers = []
        for layer_index in range(LAYERS):
            rows_low = lax.all_gather(rows_half.astype(jnp.bfloat16), "tensor", axis=0, tiled=True)
            rows_half, kept_values = layer_forward(
                rows_half,
                rows_low,
                trained[layer_index],
                layer_weights(fetched, layer_index),
                ids_all,
            )
            kept_layers.append(kept_values)
        results.append(rows_half.astype(jnp.bfloat16))
        upstream = cotangent[micro_index].astype(jnp.float32)
        for layer_index in reversed(range(LAYERS)):
            upstream, layer_grads = layer_backward(
                upstream,
                kept_layers[layer_index],
                trained[layer_index],
                layer_weights(fetched, layer_index),
                ids_all,
            )
            grad_totals[layer_index] = jax.tree.map(jnp.add, grad_totals[layer_index], layer_grads)
        input_grads.append(upstream)
    pieces = []
    for layer_index in range(LAYERS):
        scale_q_grad, scale_v_grad, bias_q_grad, bias_v_grad = grad_totals[layer_index]
        bias_q_full = lax.dynamic_update_slice_in_dim(
            jnp.zeros((D,), jnp.float32), bias_q_grad, tensor_index * feature_width, 0
        )
        bias_v_full = lax.dynamic_update_slice_in_dim(
            jnp.zeros((D,), jnp.float32), bias_v_grad, tensor_index * feature_width, 0
        )
        pieces.append(jnp.concatenate([scale_q_grad, scale_v_grad, bias_q_full, bias_v_full]))
    local_vector = jnp.concatenate(pieces).reshape(slot_of.shape[0], -1)
    full_grad = lax.psum(local_vector, ("batch", "tensor"))
    own_grad = jnp.dot(
        select, full_grad, precision=lax.Precision.HIGHEST, preferred_element_type=jnp.float32
    )
    new_one = (FIRST_BETA * first_moment + (1.0 - FIRST_BETA) * own_grad) * filled
    new_two = (SECOND_BETA * second_moment + (1.0 - SECOND_BETA) * own_grad * own_grad) * filled
    fixed_one = new_one / (1.0 - FIRST_BETA**STEP)
    fixed_two = new_two / (1.0 - SECOND_BETA**STEP)
    updated = (
        vectors
        - LEARN_RATE * (fixed_one / (jnp.sqrt(fixed_two) + ADAM_EPSILON) + WEIGHT_DECAY * vectors)
    ) * filled
    return (
        jnp.stack(results),
        jnp.stack(input_grads),
        own_grad,
        new_one,
        new_two,
        updated,
        updated.astype(jnp.bfloat16),
    )


def solution(mesh):
    return jax.shard_map(
        on_device,
        mesh=mesh,
        in_specs=(
            P(None, ("batch", "tensor"), None),
            P(None, ("batch", "tensor"), None),
            P(None, "batch", None),
            P(),
            P("batch", None),
            P("batch", None),
            P("batch", None),
            P(None, "batch", None, "tensor"),
            P(None, "tensor", "batch"),
            P(None, "batch", "tensor"),
            P(None, "tensor", "batch"),
            P("batch", None),
            P("tensor", "batch"),
            P(),
            P(),
        ),
        out_specs=(
            P(None, ("batch", "tensor"), None),
            P(None, ("batch", "tensor"), None),
            P("batch", None),
            P("batch", None),
            P("batch", None),
            P("batch", None),
            P("batch", None),
        ),
        check_vma=False,
    )
```

profile of v0, /device:TPU:0, one launch (start us, length us, event | category | flops | bytes accessed | tf_op | source)
XLA Modules:
  0.0 769.7 jit_solution(5789378090949032682)
XLA Ops:
  12.8 44.3 %all_gather.77 = f32[512,28]{1,0:T(8,128)S(1)} all-gather(f32[32,28]{1,0:T(8,128)} %param.19), channel_id=1, replica_groups=mesh['batch'=16,'tensor'=2] {'batch'}, dimensions={0}, use_global_device_ids=true | all-gather | bytes 60928 | tf_op jit(solution)/shard_map/all_gather | solution.py:237
  62.0 43.4 %all_gather.79 = bf16[384,1024]{0,1:T(8,128)(2,1)S(1)} all-gather(bf16[384,64]{0,1:T(8,128)(2,1)S(1)} %copy-done.160), channel_id=1, replica_groups=mesh['batch'=16,'tensor'=2] {'batch'}, dimensions={1}, use_global_device_ids=true | all-gather | bytes 835584 | tf_op jit(solution)/shard_map/all_gather | solution.py:285
  105.5 2.4 all-gather
  107.8 2.4 all-gather.1
  110.2 2.7 fusion.170
  118.8 28.6 %all-gather.8.cloned.1.call-done = bf16[2,768,3,384]{3,0,2,1:T(2,128)(2,1)} async-done(((bf16[2,48,3,384]{3,0,2,1:T(2,128)(2,1)}), bf16[2,768,3,384]{3,0,2,1:T(2,128)(2,1)}) %all-gather.8.cloned.1.call-update) | async-done | bytes 3538960 | tf_op jit(solution)/shard_map/all_gather | solution.py:280
  147.4 8.7 %fusion.276 = (bf16[1,768,3,384]{3,0,2,1:T(2,128)(2,1)}, bf16[1,768,3,384]{3,0,2,1:T(2,128)(2,1)}) fusion(bf16[2,768,3,384]{3,0,2,1:T(2,128)(2,1)} %all-gather.8.cloned.1.call-done), kind=kLoop, calls=%fused_computation.536 | loop fusion | bytes 7077888 | tf_op jit(solution)/shard_map/slice | solution.py:257
  156.2 11.4 %copy.118 = bf16[1,768,3,384]{1,3,2,0:T(8,128)(2,1)} copy(bf16[1,768,3,384]{3,0,2,1:T(2,128)(2,1)} %get-tuple-element.70) | data formatting | bytes 3538944
  167.6 3.0 fusion.174
  172.4 2.0 fusion.149
  179.5 25.4 %all-gather.12.cloned.1.call-done = bf16[2,384,768]{1,2,0:T(8,128)(2,1)} async-done(((bf16[2,384,48]{1,2,0:T(8,128)(2,1)}), bf16[2,384,768]{1,2,0:T(8,128)(2,1)}) %all-gather.12.cloned.1.call-update) | async-done | bytes 1179664 | tf_op jit(solution)/shard_map/all_gather | solution.py:281
  204.9 2.6 convolution_convert_fusion.3
  218.4 8.5 %reduce-scatter.25.cloned.1.call-done = bf16[256,768]{1,0:T(8,128)(2,1)} async-done(((bf16[512,768]{1,0:T(8,128)(2,1)}), bf16[256,768]{1,0:T(8,128)(2,1)}) %reduce-scatter.25.cloned.1.call-update) | async-done | bytes 393232 | tf_op jit(solution)/shard_map/reduce_scatter | solution.py:115
  230.0 2.4 all_gather.81
  232.4 78.8 %all-gather.14.cloned.1.call-done = bf16[2,768,1536]{2,1,0:T(8,128)(2,1)} async-done(((bf16[2,48,1536]{2,1,0:T(8,128)(2,1)}), bf16[2,768,1536]{2,1,0:T(8,128)(2,1)}) %all-gather.14.cloned.1.call-update) | async-done | bytes 4718608 | tf_op jit(solution)/shard_map/all_gather | solution.py:282
  311.2 10.3 %fusion.8 = (f32[512,1536]{1,0:T(8,128)}, f32[512,1536]{1,0:T(8,128)}) fusion(bf16[512,768]{1,0:T(8,128)(2,1)S(1)} %all_gather.81, bf16[2,768,1536]{2,1,0:T(8,128)(2,1)} %all-gather.14.cloned.1.call-done), kind=kOutput, calls=%fused_computation.37 | convolution fusion | flops 1256718336 | bytes 9437184 | tf_op jit(solution)/shard_map/dot_general | solution.py:123
  321.5 71.5 %all-gather.16.cloned.1.call-done = bf16[2,1536,768]{1,2,0:T(8,128)(2,1)} async-done(((bf16[2,1536,48]{1,2,0:T(8,128)(2,1)}), bf16[2,1536,768]{1,2,0:T(8,128)(2,1)}) %all-gather.16.cloned.1.call-update) | async-done | bytes 4718608 | tf_op jit(solution)/shard_map/all_gather | solution.py:283
  393.0 5.9 fusion.75
  401.0 11.5 %copy.119 = bf16[1,768,3,384]{1,3,2,0:T(8,128)(2,1)} copy(bf16[1,768,3,384]{3,0,2,1:T(2,128)(2,1)} %get-tuple-element.69) | data formatting | bytes 3538944
  416.4 2.4 all_gather.84
  418.8 2.8 all_gather.87
  423.5 9.6 %fusion.10 = (f32[512,1536]{1,0:T(8,128)S(1)}, f32[512,1536]{1,0:T(8,128)S(1)}) fusion(bf16[512,768]{1,0:T(8,128)(2,1)S(1)} %all_gather.87, bf16[2,768,1536]{2,1,0:T(8,128)(2,1)} %all-gather.14.cloned.1.call-done), kind=kOutput, calls=%fused_computation.39 | convolution fusion | flops 1256718336 | bytes 9437184 | tf_op jit(solution)/shard_map/dot_general | solution.py:123
  435.8 2.3 fusion.73
  438.3 2.4 fusion.287
  441.4 3.5 fusion.153
  453.3 5.1 reduce-scatter.21.cloned.1.call-done
  461.2 2.5 all_gather.85
  463.7 2.5 all_gather.88
  477.8 9.3 %fusion.9 = (f32[512,1536]{1,0:T(8,128)S(1)}, f32[512,1536]{1,0:T(8,128)S(1)}) fusion(bf16[512,768]{1,0:T(8,128)(2,1)S(1)} %copy-done.112, bf16[2,768,1536]{2,1,0:T(8,128)(2,1)} %all-gather.14.cloned.1.call-done), kind=kOutput, calls=%fused_computation.38 | convolution fusion | flops 1256718336 | bytes 9437184 | tf_op jit(solution)/shard_map/dot_general | solution.py:123
  489.8 4.0 fusion.74
  495.6 7.8 %reduce-scatter.23.cloned.1.call-done = bf16[256,768]{1,0:T(8,128)(2,1)} async-done(((bf16[512,768]{1,0:T(8,128)(2,1)}), bf16[256,768]{1,0:T(8,128)(2,1)}) %reduce-scatter.23.cloned.1.call-update) | async-done | bytes 393232 | tf_op jit(solution)/shard_map/reduce_scatter | solution.py:125
  503.4 2.6 fusion.271
  506.0 2.8 all_gather.89
  508.8 9.4 %fusion.11 = (f32[512,1536]{1,0:T(8,128)S(1)}, f32[512,1536]{1,0:T(8,128)S(1)}) fusion(bf16[512,768]{1,0:T(8,128)(2,1)S(1)} %all_gather.89, bf16[2,768,1536]{2,1,0:T(8,128)(2,1)} %all-gather.14.cloned.1.call-done), kind=kOutput, calls=%fused_computation.40 | convolution fusion | flops 1256718336 | bytes 9437184 | tf_op jit(solution)/shard_map/dot_general | solution.py:123
  520.8 2.3 fusion.72
  523.2 9.5 %reduce-scatter.31.cloned.1.call-done = bf16[256,768]{1,0:T(8,128)(2,1)} async-done(((bf16[512,768]{1,0:T(8,128)(2,1)}), bf16[256,768]{1,0:T(8,128)(2,1)}) %reduce-scatter.31.cloned.1.call-update) | async-done | bytes 393232 | tf_op jit(solution)/shard_map/reduce_scatter | solution.py:125
  539.0 2.5 all_gather.94
  541.5 8.2 %fusion.69 = bf16[512,768]{1,0:T(8,128)(2,1)} fusion(bf16[2,768,1536]{2,1,0:T(8,128)(2,1)} %all-gather.14.cloned.1.call-done, f32[512,1536]{1,0:T(8,128)} %copy-done.87, f32[512,1536]{1,0:T(8,128)} %copy-done.88, bf16[512,768]{1,0:T(8,128)(2,1)} %all_gather.94, bf16[2,1536,768]{1,2,0:T(8,128)(2,1)} %all-gather.16.cloned.1.call-done), kind=kOutput, calls=%fused_computation.163 | convolution fusion | flops 2427322368 | bytes 12582912 | tf_op jit(solution)/shard_map/tf,df->td/dot_general | solution.py:40
  551.1 2.5 all_gather.90
  553.6 8.5 %fusion.71 = bf16[512,768]{1,0:T(8,128)(2,1)} fusion(bf16[2,768,1536]{2,1,0:T(8,128)(2,1)} %all-gather.14.cloned.1.call-done, f32[512,1536]{1,0:T(8,128)} %copy-done.85, f32[512,1536]{1,0:T(8,128)} %copy-done.86, bf16[512,768]{1,0:T(8,128)(2,1)} %all_gather.90, bf16[2,1536,768]{1,2,0:T(8,128)(2,1)} %all-gather.16.cloned.1.call-done), kind=kOutput, calls=%fused_computation.165 | convolution fusion | flops 2427322368 | bytes 12582912 | tf_op jit(solution)/shard_map/tf,df->td/dot_general | solution.py:40
  562.8 8.9 %reduce-scatter.33.cloned.1.call-done = bf16[256,768]{1,0:T(8,128)(2,1)} async-done(((bf16[512,768]{1,0:T(8,128)(2,1)}), bf16[256,768]{1,0:T(8,128)(2,1)}) %reduce-scatter.33.cloned.1.call-update) | async-done | bytes 393232 | tf_op jit(solution)/shard_map/reduce_scatter | solution.py:168
  571.7 2.6 multiply_reduce_fusion.17
  575.7 3.5 fusion.267
  579.3 2.5 all_gather.95
  586.7 2.6 fusion.80
  589.3 3.0 fusion.81
  593.0 2.4 all_gather.91
  606.0 2.2 fusion.212
  615.0 4.0 fusion.84
  622.4 2.8 add_convert_fusion.11
  625.8 9.0 %reduce-scatter.35.cloned.1.call-done = bf16[256,768]{1,0:T(8,128)(2,1)} async-done(((bf16[512,768]{1,0:T(8,128)(2,1)}), bf16[256,768]{1,0:T(8,128)(2,1)}) %reduce-scatter.35.cloned.1.call-update) | async-done | bytes 393232 | tf_op jit(solution)/shard_map/reduce_scatter | solution.py:201
  634.9 2.1 multiply_reduce_fusion.16
  638.2 2.9 fusion.265
  642.0 2.4 all_gather.92
  644.4 8.1 %fusion.70 = bf16[512,768]{1,0:T(8,128)(2,1)} fusion(bf16[2,768,1536]{2,1,0:T(8,128)(2,1)} %all-gather.14.cloned.1.call-done, f32[512,1536]{1,0:T(8,128)} %get-tuple-element.121, f32[512,1536]{1,0:T(8,128)} %get-tuple-element.122, bf16[512,768]{1,0:T(8,128)(2,1)S(1)} %all_gather.92, bf16[2,1536,768]{1,2,0:T(8,128)(2,1)} %all-gather.16.cloned.1.call-done), kind=kOutput, calls=%fused_computation.164 | convolution fusion | flops 2427322368 | bytes 12582912 | tf_op jit(solution)/shard_map/tf,df->td/dot_general | solution.py:40
  652.6 2.4 all_gather.96
  655.0 8.1 %fusion.68 = bf16[512,768]{1,0:T(8,128)(2,1)} fusion(bf16[2,768,1536]{2,1,0:T(8,128)(2,1)} %all-gather.14.cloned.1.call-done, f32[512,1536]{1,0:T(8,128)} %copy-done.83, f32[512,1536]{1,0:T(8,128)} %copy-done.84, bf16[512,768]{1,0:T(8,128)(2,1)S(1)} %all_gather.96, bf16[2,1536,768]{1,2,0:T(8,128)(2,1)} %all-gather.16.cloned.1.call-done), kind=kOutput, calls=%fused_computation.162 | convolution fusion | flops 2427322368 | bytes 12582912 | tf_op jit(solution)/shard_map/tf,df->td/dot_general | solution.py:40
  663.3 2.2 pad_maximum_fusion.1
  670.4 3.4 reduce-scatter.45.cloned.1.call-done
  673.9 2.8 multiply_reduce_fusion.15
  678.0 2.5 all_gather.93
  688.1 2.5 all_gather.97
  713.3 2.7 add_convert_fusion.8
  716.5 41.6 %psum.7 = f32[256,28]{1,0:T(8,128)S(1)} all-reduce(f32[256,28]{1,0:T(8,128)S(1)} %reshape.520), channel_id=1, replica_groups=mesh['batch'=16,'tensor'=2] {'batch','tensor'}, use_global_device_ids=true, to_apply=%region_81.82 | all-reduce | flops 7168 | bytes 57344 | tf_op jit(solution)/shard_map/psum | solution.py:323
  (693 shorter events, 157.0 us)
Async XLA Ops:
  7.2 54.9 %copy-start.160 = (bf16[384,64]{0,1:T(8,128)(2,1)S(1)}, bf16[384,64]{0,1:T(8,128)(2,1)}, u32[]{:S(2)}) copy-start(bf16[384,64]{0,1:T(8,128)(2,1)} %param.27) | copy-start | bytes 147460
  7.2 98.2 %copy-start.4 = (bf16[2,256,768]{2,1,0:T(8,128)(2,1)S(1)}, bf16[2,256,768]{2,1,0:T(8,128)(2,1)}, u32[]{:S(2)}) copy-start(bf16[2,256,768]{2,1,0:T(8,128)(2,1)} %param.15) | copy-start | bytes 2359300
  7.2 103.0 %all-gather.10.cloned.1.call-start = ((), (), s32[]{:S(2)}) async-start(), calls=%async_computation.17 | async-start | bytes 1671168 | tf_op jit(solution)/shard_map/all_gather | solution.py:284
  7.9 139.5 %all-gather.8.cloned.1.call-start = ((), (), s32[]{:S(2)}) async-start(), calls=%async_computation.16 | async-start | bytes 3760128 | tf_op jit(solution)/shard_map/all_gather | solution.py:280
  9.8 195.1 %all-gather.12.cloned.1.call-start = ((), (), s32[]{:S(2)}) async-start(), calls=%async_computation.18 | async-start | bytes 1253376 | tf_op jit(solution)/shard_map/all_gather | solution.py:281
  10.5 206.7 %reduce-scatter.17.cloned.1.call-start = ((), (), s32[]{:S(2)}) async-start(), calls=%async_computation.19 | async-start | bytes 1179648 | tf_op jit(solution)/shard_map/reduce_scatter | solution.py:115
  58.7 57.3 %copy-start.134 = (f32[1024]{0:T(1024)}, f32[1024]{0:T(1024)S(1)}, u32[]{:S(2)}) copy-start(f32[1024]{0:T(1024)S(1)} %get-tuple-element.100) | copy-start | bytes 12292
  58.7 113.2 %copy-start.132 = (f32[1024]{0:T(1024)}, f32[1024]{0:T(1024)S(1)}, u32[]{:S(2)}) copy-start(f32[1024]{0:T(1024)S(1)} %get-tuple-element.99) | copy-start | bytes 12292
  62.0 109.9 %copy-start.174 = (f32[384]{0:T(512)}, f32[384]{0:T(512)S(1)}, u32[]{:S(2)}) copy-start(f32[384]{0:T(512)S(1)} %dynamic_slice.13) | copy-start | bytes 4612
  62.0 109.9 %copy-start.172 = (f32[384]{0:T(512)}, f32[384]{0:T(512)S(1)}, u32[]{:S(2)}) copy-start(f32[384]{0:T(512)S(1)} %dynamic_slice.12) | copy-start | bytes 4612
  114.9 57.0 %copy-start.49 = (f32[512,384]{0,1:T(8,128)}, f32[512,384]{0,1:T(8,128)S(1)}, u32[]{:S(2)}) copy-start(f32[512,384]{0,1:T(8,128)S(1)} %fusion.104) | copy-start | bytes 2359300
  116.6 55.3 %copy-start.51 = (f32[512,384]{0,1:T(8,128)}, f32[512,384]{0,1:T(8,128)S(1)}, u32[]{:S(2)}) copy-start(f32[512,384]{0,1:T(8,128)S(1)} %fusion.100) | copy-start | bytes 2359300
  172.4 35.4 %copy-start.72 = (bf16[512,1,384]{0,2,1:T(8,128)(2,1)}, bf16[512,1,384]{0,2,1:T(8,128)(2,1)S(1)}, u32[]{:S(2)}) copy-start(bf16[512,1,384]{0,2,1:T(8,128)(2,1)S(1)} %slice.469) | copy-start | bytes 1179652
  178.3 29.4 %copy-start.78 = (bf16[512,384]{0,1:T(8,128)(2,1)S(1)}, bf16[512,384]{0,1:T(8,128)(2,1)}, u32[]{:S(2)}) copy-start(bf16[512,384]{0,1:T(8,128)(2,1)} %get-tuple-element.77) | copy-start | bytes 1179652
  178.3 29.5 %copy-start.90 = (pred[512,512]{0,1:T(8,128)(4,1)S(1)}, pred[512,512]{0,1:T(8,128)(4,1)}, u32[]{:S(2)}) copy-start(pred[512,512]{0,1:T(8,128)(4,1)} %broadcast_compare_fusion) | copy-start | bytes 786436
  207.5 19.5 %reduce-scatter.25.cloned.1.call-start = ((), (), s32[]{:S(2)}) async-start(), calls=%async_computation.25 | async-start | bytes 1179648 | tf_op jit(solution)/shard_map/reduce_scatter | solution.py:115
  214.6 96.6 %all-gather.14.cloned.1.call-start = ((), (), s32[]{:S(2)}) async-start(), calls=%async_computation.20 | async-start | bytes 5013504 | tf_op jit(solution)/shard_map/all_gather | solution.py:282
  215.2 177.8 %all-gather.16.cloned.1.call-start = ((), (), s32[]{:S(2)}) async-start(), calls=%async_computation.21 | async-start | bytes 5013504 | tf_op jit(solution)/shard_map/all_gather | solution.py:283
  215.9 197.1 %reduce-scatter.19.cloned.1.call-start = ((), (), s32[]{:S(2)}) async-start(), calls=%async_computation.22 | async-start | bytes 1179648 | tf_op jit(solution)/shard_map/reduce_scatter | solution.py:125
  216.6 235.1 %copy-start.127 = (f32[768]{0:T(1024)}, f32[768]{0:T(1024)S(1)}, u32[]{:S(2)}) copy-start(f32[768]{0:T(1024)S(1)} %get-tuple-element.25) | copy-start | bytes 9220
  216.6 277.3 %copy-start.129 = (f32[768]{0:T(1024)}, f32[768]{0:T(1024)S(1)}, u32[]{:S(2)}) copy-start(f32[768]{0:T(1024)S(1)} %get-tuple-element.24) | copy-start | bytes 9220
  216.6 316.2 %copy-start.131 = (f32[768]{0:T(1024)}, f32[768]{0:T(1024)S(1)}, u32[]{:S(2)}) copy-start(f32[768]{0:T(1024)S(1)} %get-tuple-element.26) | copy-start | bytes 9220
  217.2 12.7 %copy-start.145 = (f32[768]{0:T(1024)}, f32[768]{0:T(1024)S(1)}, u32[]{:S(2)}) copy-start(f32[768]{0:T(1024)S(1)} %get-tuple-element.29) | copy-start | bytes 9220
  230.0 182.4 %copy-start.198 = (f32[256]{0:T(256)}, f32[256]{0:T(256)S(1)}, u32[]{:S(2)}) copy-start(f32[256]{0:T(256)S(1)} %get-tuple-element.88) | copy-start | bytes 3076
  398.9 14.2 %copy-start.27 = (bf16[256,768]{1,0:T(8,128)(2,1)S(1)}, bf16[256,768]{1,0:T(8,128)(2,1)}, u32[]{:S(2)}) copy-start(bf16[256,768]{1,0:T(8,128)(2,1)} %reduce-scatter.17.cloned.1.call-done) | copy-start | bytes 1179652
  398.9 14.2 %copy-start.29 = (bf16[256,768]{1,0:T(8,128)(2,1)S(1)}, bf16[256,768]{1,0:T(8,128)(2,1)}, u32[]{:S(2)}) copy-start(bf16[256,768]{1,0:T(8,128)(2,1)} %reduce-scatter.25.cloned.1.call-done) | copy-start | bytes 1179652
  398.9 52.8 %reduce-scatter.27.cloned.1.call-start = ((), (), s32[]{:S(2)}) async-start(), calls=%async_computation.26 | async-start | bytes 1179648 | tf_op jit(solution)/shard_map/reduce_scatter | solution.py:125
  401.0 68.4 %copy-start.136 = (f32[1024]{0:T(1024)}, f32[1024]{0:T(1024)S(1)}, u32[]{:S(2)}) copy-start(f32[1024]{0:T(1024)S(1)} %get-tuple-element.95) | copy-start | bytes 12292
  421.5 14.3 %slice-start.8 = ((s8[4718592]{0:T(1024)(128)(4,1)}), s8[4194304]{0:T(1024)(128)(4,1)S(1)}, s32[]{:S(2)}) async-start(s8[4718592]{0:T(1024)(128)(4,1)} %bitcast.393), calls=%async_computation.45 | async-start | bytes 8388608
  438.2 20.3 %reduce-scatter.21.cloned.1.call-start = ((), (), s32[]{:S(2)}) async-start(), calls=%async_computation.23 | async-start | bytes 1179648 | tf_op jit(solution)/shard_map/reduce_scatter | solution.py:115
  451.6 42.3 %reduce-scatter.29.cloned.1.call-start = ((), (), s32[]{:S(2)}) async-start(), calls=%async_computation.27 | async-start | bytes 1179648 | tf_op jit(solution)/shard_map/reduce_scatter | solution.py:115
  453.1 40.9 %copy-start.163 = (f32[256]{0:T(256)}, f32[256]{0:T(256)S(1)}, u32[]{:S(2)}) copy-start(f32[256]{0:T(256)S(1)} %broadcast_multiply_fusion.2) | copy-start | bytes 3076
  453.3 40.6 %copy-start.181 = (f32[256]{0:T(256)}, f32[256]{0:T(256)S(1)}, u32[]{:S(2)}) copy-start(f32[256]{0:T(256)S(1)} %fusion.236) | copy-start | bytes 3076
  460.0 43.4 %copy-start.165 = (f32[256]{0:T(256)}, f32[256]{0:T(256)S(1)}, u32[]{:S(2)}) copy-start(f32[256]{0:T(256)S(1)} %broadcast_multiply_fusion.5) | copy-start | bytes 3076
  460.3 43.1 %copy-start.182 = (f32[256]{0:T(256)}, f32[256]{0:T(256)S(1)}, u32[]{:S(2)}) copy-start(f32[256]{0:T(256)S(1)} %fusion.233) | copy-start | bytes 3076
  477.8 25.6 %reduce-scatter.23.cloned.1.call-start = ((), (), s32[]{:S(2)}) async-start(), calls=%async_computation.24 | async-start | bytes 1179648 | tf_op jit(solution)/shard_map/reduce_scatter | solution.py:125
  493.8 38.9 %reduce-scatter.31.cloned.1.call-start = ((), (), s32[]{:S(2)}) async-start(), calls=%async_computation.28 | async-start | bytes 1179648 | tf_op jit(solution)/shard_map/reduce_scatter | solution.py:125
  495.3 37.4 %copy-start.166 = (f32[256]{0:T(256)}, f32[256]{0:T(256)S(1)}, u32[]{:S(2)}) copy-start(f32[256]{0:T(256)S(1)} %broadcast_multiply_fusion.1) | copy-start | bytes 3076
  495.5 22.6 %copy-start.203 = (f32[256]{0:T(256)}, f32[256]{0:T(256)S(1)}, u32[]{:S(2)}) copy-start(f32[256]{0:T(256)S(1)} %multiply_reduce_fusion.19) | copy-start | bytes 3076
  495.6 37.2 %copy-start.183 = (f32[256]{0:T(256)}, f32[256]{0:T(256)S(1)}, u32[]{:S(2)}) copy-start(f32[256]{0:T(256)S(1)} %fusion.237) | copy-start | bytes 3076
  503.4 17.4 %slice-start.10 = ((s8[4718592]{0:T(1024)(128)(4,1)}), s8[4194304]{0:T(1024)(128)(4,1)S(1)}, s32[]{:S(2)}) async-start(s8[4718592]{0:T(1024)(128)(4,1)} %bitcast.395), calls=%async_computation.47 | async-start | bytes 8388608
  520.8 13.4 %copy-start.169 = (f32[768]{0:T(1024)S(1)}, f32[768]{0:T(1024)}, u32[]{:S(2)}) copy-start(f32[768]{0:T(1024)} %get-tuple-element.23) | copy-start | bytes 9220
  523.1 13.0 %copy-start.186 = (f32[768]{0:T(1024)S(1)}, f32[768]{0:T(1024)}, u32[]{:S(2)}) copy-start(f32[768]{0:T(1024)} %get-tuple-element.27) | copy-start | bytes 9220
  523.2 39.6 %reduce-scatter.41.cloned.1.call-start = ((), (), s32[]{:S(2)}) async-start(), calls=%async_computation.33 | async-start | bytes 1179648 | tf_op jit(solution)/shard_map/reduce_scatter | solution.py:168
  549.7 21.9 %reduce-scatter.33.cloned.1.call-start = ((), (), s32[]{:S(2)}) async-start(), calls=%async_computation.29 | async-start | bytes 1179648 | tf_op jit(solution)/shard_map/reduce_scatter | solution.py:168
  562.1 63.7 %reduce-scatter.43.cloned.1.call-start = ((), (), s32[]{:S(2)}) async-start(), calls=%async_computation.34 | async-start | bytes 1179648 | tf_op jit(solution)/shard_map/reduce_scatter | solution.py:201
  562.8 12.8 %copy-start.107 = (bf16[256,768]{1,0:T(8,128)(2,1)S(1)}, bf16[256,768]{1,0:T(8,128)(2,1)}, u32[]{:S(2)}) copy-start(bf16[256,768]{1,0:T(8,128)(2,1)} %reduce-scatter.41.cloned.1.call-done) | copy-start | bytes 1179652
  583.5 27.9 %copy-start.55 = (bf16[6,64,512]{2,1,0:T(8,128)(2,1)}, bf16[6,64,512]{2,1,0:T(8,128)(2,1)S(1)}, u32[]{:S(2)}) copy-start(bf16[6,64,512]{2,1,0:T(8,128)(2,1)S(1)} %fusion.90) | copy-start | bytes 1179652
  613.1 21.7 %reduce-scatter.35.cloned.1.call-start = ((), (), s32[]{:S(2)}) async-start(), calls=%async_computation.30 | async-start | bytes 1179648 | tf_op jit(solution)/shard_map/reduce_scatter | solution.py:201
  622.3 12.5 %copy-start.33 = (f32[256,768]{1,0:T(8,128)S(1)}, f32[256,768]{1,0:T(8,128)}, u32[]{:S(2)}) copy-start(f32[256,768]{1,0:T(8,128)} %copy-done.32) | copy-start | bytes 2359300
  622.3 12.5 %copy-start.130 = (f32[768]{0:T(1024)S(1)}, f32[768]{0:T(1024)}, u32[]{:S(2)}) copy-start(f32[768]{0:T(1024)} %copy-done.129) | copy-start | bytes 9220
  625.1 45.3 %reduce-scatter.37.cloned.1.call-start = ((), (), s32[]{:S(2)}) async-start(), calls=%async_computation.31 | async-start | bytes 1179648 | tf_op jit(solution)/shard_map/reduce_scatter | solution.py:168
  652.4 21.4 %reduce-scatter.45.cloned.1.call-start = ((), (), s32[]{:S(2)}) async-start(), calls=%async_computation.35 | async-start | bytes 1179648 | tf_op jit(solution)/shard_map/reduce_scatter | solution.py:168
  663.1 95.9 %reduce-scatter.39.cloned.1.call-start = ((), (), s32[]{:S(2)}) async-start(), calls=%async_computation.32 | async-start | bytes 1179648 | tf_op jit(solution)/shard_map/reduce_scatter | solution.py:201
  666.8 14.2 %slice-start.2 = ((s8[6291456]{0:T(1024)(128)(4,1)}), s8[2097152]{0:T(1024)(128)(4,1)S(1)}, s32[]{:S(2)}) async-start(s8[6291456]{0:T(1024)(128)(4,1)} %bitcast.387), calls=%async_computation.39 | async-start | bytes 4194304
  706.1 54.1 %reduce-scatter.47.cloned.1.call-start = ((), (), s32[]{:S(2)}) async-start(), calls=%async_computation.36 | async-start | bytes 1179648 | tf_op jit(solution)/shard_map/reduce_scatter | solution.py:201
  713.2 44.9 %copy-start.152 = (f32[32,28]{1,0:T(8,128)S(1)}, f32[32,28]{1,0:T(8,128)}, u32[]{:S(2)}) copy-start(f32[32,28]{1,0:T(8,128)} %param.19) | copy-start | bytes 10756
  713.2 44.9 %copy-start.189 = (s32[256]{0:T(256)S(1)}, s32[256]{0:T(256)}, u32[]{:S(2)}) copy-start(s32[256]{0:T(256)} %copy-done.187) | copy-start | bytes 3076
  713.2 44.9 %copy-start.190 = (f32[32,28]{1,0:T(8,128)S(1)}, f32[32,28]{1,0:T(8,128)}, u32[]{:S(2)}) copy-start(f32[32,28]{1,0:T(8,128)} %param.21) | copy-start | bytes 10756
  713.2 44.9 %copy-start.191 = (f32[32,28]{1,0:T(8,128)S(1)}, f32[32,28]{1,0:T(8,128)}, u32[]{:S(2)}) copy-start(f32[32,28]{1,0:T(8,128)} %param.20) | copy-start | bytes 10756
  713.3 44.9 %copy-start.207 = (pred[256]{0:T(512)(128)(4,1)S(1)}, pred[256]{0:T(512)(128)(4,1)}, u32[]{:S(2)}) copy-start(pred[256]{0:T(512)(128)(4,1)} %get-tuple-element.109) | copy-start | bytes 772
  713.3 44.9 %copy-start.209 = (f32[32]{0:T(128)S(1)}, f32[32]{0:T(128)}, u32[]{:S(2)}) copy-start(f32[32]{0:T(128)} %convert_reduce_fusion.1) | copy-start | bytes 388
  713.3 45.8 %copy-start.44 = (f32[256,768]{1,0:T(8,128)S(1)}, f32[256,768]{1,0:T(8,128)}, u32[]{:S(2)}) copy-start(f32[256,768]{1,0:T(8,128)} %copy-done.43) | copy-start | bytes 2359300
  716.0 44.2 %copy-start.42 = (f32[256,768]{1,0:T(8,128)S(1)}, f32[256,768]{1,0:T(8,128)}, u32[]{:S(2)}) copy-start(f32[256,768]{1,0:T(8,128)} %copy-done.41) | copy-start | bytes 2359300
  (179 other events, 732.5 us)
Sparse Core Ops, SparseCore 0:
  10.8 64.5 all-gather.9
  78.2 69.2 all-gather.7
  150.1 54.7 all-gather.11
  207.6 7.1 reduce-scatter.16
  217.6 9.3 reduce-scatter.24
  229.5 81.6 all-gather.13
  313.8 79.0 all-gather.15
  399.0 6.8 reduce-scatter.18
  438.3 6.8 reduce-scatter.26
  451.7 6.6 reduce-scatter.20
  477.9 9.3 reduce-scatter.28
  494.0 9.4 reduce-scatter.22
  523.3 9.3 reduce-scatter.30
  549.9 9.4 reduce-scatter.40
  562.2 9.3 reduce-scatter.32
  613.2 9.4 reduce-scatter.42
  625.4 9.3 reduce-scatter.34
  652.6 9.4 reduce-scatter.36
  664.3 9.4 reduce-scatter.44
  706.2 9.3 reduce-scatter.38
  718.6 9.3 reduce-scatter.46
where the time goes:
time: 781 us; the launch traced here: 770 us
  waiting for transfers between devices  259 us (33%)
  matrix products  190 us (24%)
  blocking collectives  169 us (22%)
  other arithmetic  69.1 us (9%)
  local copies, waits for them, and re-layouts  63.3 us (8%)
  between operations  17.7 us (2%)
    dot_general x68, matrix products, product(): return jnp.einsum(form, left, right, preferred_element_type=jnp.float32)  125 us
    all_gather x1, waiting for transfers between devices, on_device(): lax.all_gather(weight_up, 'batch', axis=1, tiled=True)  78.8 us
    all_gather x1, waiting for transfers between devices, on_device(): lax.all_gather(weight_down, 'batch', axis=2, tiled=True)  71.5 us
    unnamed x450, local copies, waits for them, and re-layouts  47.7 us
    all_gather x1, blocking collectives, on_device(): all_slots = lax.all_gather(vectors, 'batch', axis=0, tiled=True)  44.3 us
    all_gather x1, blocking collectives, on_device(): lax.all_gather(basis_b, 'batch', axis=1, tiled=True)  43.4 us
    psum x1, blocking collectives, on_device(): full_grad = lax.psum(local_vector, ('batch', 'tensor'))  41.6 us
    dot_general x4, matrix products, layer_forward(): before = jnp.dot(middle_low, weight_up, preferred_element_type=jnp.float32)  38.6 us
  transfers between devices with their start and end apart: 21, of which 11 were waited for; matrix products, arithmetic and copies ran while one was open for 20% of the time, Pallas kernels for 0%

commit v1 on v0

v1 whole, which is shorter than its diff:
```python
import functools

import jax
import jax.numpy as jnp
from jax import lax
from jax.experimental import pallas as pl
from jax.experimental.pallas import tpu as pltpu
from jax.sharding import PartitionSpec as P

D = 768
HDIM = 64
R = 1024
LAYERS = 2
STEP = 10
HALF = 384
GROUPS = 16
BLOCKS = 24
CHUNKS = 13
LAG = 2

EPSILON = 1e-05
SCORE_SCALE = 0.125
MASKED_SCORE = -1000000000.0
LEARN_RATE = 0.3
WEIGHT_DECAY = 0.01
FIRST_BETA = 0.5
SECOND_BETA = 0.5
ADAM_EPSILON = 1e-08
MESH = pl.DeviceIdType.MESH

ARRIVALS = ["Si", "Sj", "Sf", "Dj", "Df", "Xo", "Xi", "Xj", "Xf", "Yo", "Yi", "Yj", "Yf", "Dxo", "Dxi", "Dyo", "Dyi"]
SLOT = {name: index for index, name in enumerate(ARRIVALS)}
FROM_SIBLING = len(ARRIVALS)
TO_SIBLING, TO_X, TO_Y, TO_IN, TO_OUT, LOCAL = range(6)
DEPTHS = 7


class Gather:
    def __init__(self, sub, pack_wide, pack, wide, full, send_sem, recv_sem):
        self.sub = sub
        self.pack_wide, self.pack, self.wide, self.full = pack_wide, pack, wide, full
        self.send_sem, self.recv_sem = send_sem, recv_sem
        batch = lax.axis_index("batch")
        self.core = lax.axis_index("tensor")
        group = batch // sub
        self.lane = batch % sub
        z, p = group // 4, group % 4
        inward = 1 - 2 * (z // 2)
        self.middle = ((z + 1) // 2) % 2
        plane_i, plane_j = z + inward, z + 2 * inward
        plane_f = 6 - z - plane_i - plane_j
        self.planes = {"o": z, "i": plane_i, "j": plane_j, "f": plane_f}
        col_x, col_y = p + 1 - 2 * (p % 2), p + 2 - 4 * (p // 2)
        self.cols = {"S": p, "X": col_x, "Y": col_y, "D": 3 - p}
        self.sibling = (batch, 1 - self.core)
        self.to_x = self.device(z, col_x)
        self.to_y = self.device(z, col_y)
        self.to_in = self.device(plane_i, p)
        self.to_out = self.device(plane_f, p)

    def device(self, plane, col):
        return ((plane * 4 + col) * self.sub + self.lane, self.core)

    def barrier(self):
        semaphore = pltpu.get_barrier_semaphore()
        for device in (self.sibling, self.to_x, self.to_y, self.to_in):
            pl.semaphore_signal(semaphore, inc=1, device_id=device, device_id_type=MESH)

        @pl.when(self.middle == 1)
        def _():
            pl.semaphore_signal(semaphore, inc=1, device_id=self.to_out, device_id_type=MESH)
            pl.semaphore_wait(semaphore, 5)

        @pl.when(self.middle == 0)
        def _():
            pl.semaphore_wait(semaphore, 4)

    def rows(self, chunk, half, start, count, blocks=(0, 2)):
        ref, size, base = (self.wide, 64, 0) if chunk == 0 else (self.full, 48, 2 * (chunk - 1))
        first = pl.multiple_of(start * size, 16) if not isinstance(start, int) else start * size
        return ref.at[half, pl.ds(base + blocks[0], blocks[1]), pl.ds(first, count * size)]

    def shard(self, chunk, half, col, plane, blocks=(0, 2)):
        return self.rows(chunk, half, self.planes[plane] * 4 + self.cols[col], 1, blocks)

    def copy(self, chunk, source, target, device, send, slot):
        pltpu.make_async_remote_copy(
            src_ref=source,
            dst_ref=target,
            send_sem=self.send_sem.at[chunk, send],
            recv_sem=self.recv_sem.at[chunk, slot],
            device_id=device,
            device_id_type=MESH,
        ).start()

    def push(self, chunk, col, plane, moves, blocks=(0, 2), sibling=True, source=None):
        region = self.shard(chunk, self.core, col, plane, blocks)
        source = region if source is None else source
        for device, send, slot in moves:
            slot = SLOT[slot] if isinstance(slot, str) else slot
            self.copy(chunk, source, region, device, send, slot)
        if sibling:
            self.copy(chunk, source, region, self.sibling, TO_SIBLING, FROM_SIBLING)

    def take(self, chunk, name):
        blocks = {"x": (0, 1), "y": (1, 1)}.get(name[1:-1], (0, 2))
        region = self.shard(chunk, self.core, name[0], name[-1], blocks)
        pltpu.make_async_remote_copy(
            src_ref=region,
            dst_ref=region,
            send_sem=self.send_sem.at[chunk, TO_X],
            recv_sem=self.recv_sem.at[chunk, SLOT[name]],
            device_id=self.to_x,
            device_id_type=MESH,
        ).wait_recv()

    def when_middle(self, action):
        pl.when(self.middle == 1)(action)

    def when_end(self, action):
        pl.when(self.middle == 0)(action)

    def local(self, chunk):
        source = self.pack_wide if chunk == 0 else self.pack.at[pl.ds(2 * (chunk - 1), 2)]
        return pltpu.make_async_copy(
            source, self.shard(chunk, self.core, "S", "o"), self.send_sem.at[chunk, LOCAL]
        )

    def step(self, chunk, depth):
        to_x, to_y = (self.to_x, TO_X), (self.to_y, TO_Y)
        to_in, to_out = (self.to_in, TO_IN), (self.to_out, TO_OUT)
        if depth == 0:
            source = self.pack_wide if chunk == 0 else self.pack.at[pl.ds(2 * (chunk - 1), 2)]
            arrival = self.middle * SLOT["Si"] + (1 - self.middle) * SLOT["Sf"]
            self.push(chunk, "S", "o", [(*to_in, arrival), (*to_x, "Xo"), (*to_y, "Yo")], source=source)

            @self.when_middle
            def _():
                self.push(chunk, "S", "o", [(*to_out, "Si")], sibling=False, source=source)

            self.local(chunk).start()
        elif depth == 1:
            self.take(chunk, "Si")

            @self.when_middle
            def _():
                self.push(chunk, "S", "i", [(*to_out, "Sj")], sibling=False)
                self.take(chunk, "Sf")
                self.push(chunk, "S", "f", [(*to_in, "Sj"), (*to_x, "Xf"), (*to_y, "Yf")])

            self.push(chunk, "S", "i", [(*to_x, "Xi"), (*to_y, "Yi")])
            self.cross(chunk, "o")
        elif depth == 2:
            self.take(chunk, "Sj")

            @self.when_middle
            def _():
                self.push(chunk, "S", "j", [(*to_out, "Sf")], sibling=False)

            self.push(chunk, "S", "j", [(*to_x, "Xj"), (*to_y, "Yj")])
            self.take(chunk, "Dxo")
            self.take(chunk, "Dyo")

            @self.when_end
            def _():
                self.push(chunk, "D", "o", [(*to_in, "Df")], sibling=False)

            self.push(chunk, "D", "o", [])
            self.cross(chunk, "i")

            @self.when_middle
            def _():
                self.land(chunk, "Xf", "Yf")
        elif depth == 3:
            @self.when_end
            def _():
                self.take(chunk, "Sf")
                self.push(chunk, "S", "f", [(*to_x, "Xf"), (*to_y, "Yf")])

            self.take(chunk, "Dxi")
            self.take(chunk, "Dyi")

            @self.when_middle
            def _():
                self.push(chunk, "D", "i", [(*to_out, "Dj")], sibling=False)
                self.take(chunk, "Df")
                self.push(chunk, "D", "f", [(*to_in, "Dj")])

            self.push(chunk, "D", "i", [])
            self.land(chunk, "Xj", "Yj")
        elif depth == 4:
            self.take(chunk, "Dj")

            @self.when_middle
            def _():
                self.push(chunk, "D", "j", [(*to_out, "Df")], sibling=False)

            self.push(chunk, "D", "j", [])

            @self.when_end
            def _():
                self.land(chunk, "Xf", "Yf")
        elif depth == 5:
            @self.when_end
            def _():
                self.land(chunk, "Df")
        else:
            self.local(chunk).wait()
            whole = self.rows(chunk, 1 - self.core, 0, GROUPS)
            pltpu.make_async_remote_copy(
                src_ref=whole,
                dst_ref=whole,
                send_sem=self.send_sem.at[chunk, TO_SIBLING],
                recv_sem=self.recv_sem.at[chunk, FROM_SIBLING],
                device_id=self.sibling,
                device_id_type=MESH,
            ).wait_recv()

    def cross(self, chunk, plane):
        self.take(chunk, "X" + plane)
        self.push(chunk, "X", plane, [(self.to_y, TO_Y, "Dy" + plane)], (1, 1), sibling=False)
        self.push(chunk, "X", plane, [])
        self.take(chunk, "Y" + plane)
        self.push(chunk, "Y", plane, [(self.to_x, TO_X, "Dx" + plane)], (0, 1), sibling=False)
        self.push(chunk, "Y", plane, [])

    def land(self, chunk, *names):
        for name in names:
            self.take(chunk, name)
            self.push(chunk, name[0], name[1], [])

    def sent(self, chunk, send, shards):
        region = self.rows(chunk, self.core, 0, shards)
        pltpu.make_async_remote_copy(
            src_ref=region,
            dst_ref=region,
            send_sem=self.send_sem.at[chunk, send],
            recv_sem=self.recv_sem.at[chunk, FROM_SIBLING],
            device_id=self.sibling,
            device_id_type=MESH,
        ).wait_send()

    def finish(self):
        for chunk in range(CHUNKS):
            self.sent(chunk, TO_SIBLING, GROUPS)
            self.sent(chunk, TO_X, 5)
            self.sent(chunk, TO_Y, 5)

        @self.when_middle
        def _():
            for chunk in range(CHUNKS):
                self.sent(chunk, TO_IN, 3)
                self.sent(chunk, TO_OUT, 5)

        @self.when_end
        def _():
            for chunk in range(CHUNKS):
                self.sent(chunk, TO_IN, 2)

    def tick(self, number):
        for depth in range(DEPTHS):
            chunk, rest = divmod(number - depth, LAG)
            if rest == 0 and 0 <= chunk < CHUNKS:
                self.step(chunk, depth)


TICKS = LAG * (CHUNKS - 1) + DEPTHS


def gather_kernel(sub, pack_wide, pack, wide, full, send_sem, recv_sem):
    gather = Gather(sub, pack_wide, pack, wide, full, send_sem, recv_sem)
    gather.barrier()
    for number in range(TICKS):
        gather.tick(number)
    gather.finish()


def gather_weights(sub, pack_wide, pack):
    return pl.pallas_call(
        functools.partial(gather_kernel, sub),
        out_shape=(
            jax.ShapeDtypeStruct((2, 2, R, HALF), jnp.bfloat16),
            jax.ShapeDtypeStruct((2, BLOCKS, D, HALF), jnp.bfloat16),
        ),
        in_specs=[pl.BlockSpec(memory_space=pl.ANY)] * 2,
        out_specs=[pl.BlockSpec(memory_space=pl.ANY)] * 2,
        scratch_shapes=[
            pltpu.SemaphoreType.DMA((CHUNKS, 6)),
            pltpu.SemaphoreType.DMA((CHUNKS, len(ARRIVALS) + 1)),
        ],
        compiler_params=pltpu.CompilerParams(collective_id=0, has_side_effects=True),
    )(pack_wide, pack)


def pack_weights(sub, weight_in, weight_out, weight_up, weight_down, basis_a, basis_b):
    core = lax.axis_index("tensor")
    rows_in = weight_in.shape[1]
    blocks = []
    for layer in range(LAYERS):
        ins = [weight_in[layer, :, part] for part in range(3)]
        outs = weight_out[layer].T
        ups = weight_up[layer].reshape(rows_in, 4, HALF)
        downs = weight_down[layer].T.reshape(rows_in, 4, HALF)
        blocks += ins + [outs]
        for part in range(4):
            blocks += [ups[:, part], downs[:, part]]
    pack = jnp.stack(blocks)
    pack_wide = jnp.stack([lax.dynamic_slice_in_dim(basis_a, core * HALF, HALF, 1), basis_b.T])
    if sub > 1:
        group = lax.axis_index("batch") // sub
        pack = lax.all_gather(pack, "batch", axis=1, tiled=True)
        pack = lax.dynamic_slice_in_dim(pack, group * (D // GROUPS), D // GROUPS, 1)
        pack_wide = lax.all_gather(pack_wide, "batch", axis=1, tiled=True)
        pack_wide = lax.dynamic_slice_in_dim(pack_wide, group * (R // GROUPS), R // GROUPS, 1)
    return pack_wide, pack


def normalize(values, gain_row, offset):
    center = values - jnp.mean(values, axis=-1, keepdims=True)
    spread = jnp.mean(center * center, axis=-1, keepdims=True)
    return center * lax.rsqrt(spread + EPSILON) * gain_row + offset


def norm_back(values, gain_row, offset, upstream):
    _, pullback = jax.vjp(lambda argument: normalize(argument, gain_row, offset), values)
    return pullback(upstream)[0]


def gelu_back(before, upstream):
    _, pullback = jax.vjp(lambda argument: jax.nn.gelu(argument, approximate=False), before)
    return pullback(upstream)[0]


def product(left, right, form):
    return jnp.einsum(form, left, right, preferred_element_type=jnp.float32)


def low(values):
    return values.astype(jnp.bfloat16)


def segment_ids(doc_sizes, total_rows):
    doc_ends = jnp.cumsum(doc_sizes)
    places = jnp.arange(total_rows, dtype=jnp.int32)
    return jnp.sum((doc_ends[None, :] <= places[:, None]).astype(jnp.int32), axis=1)


def owner_tables(owners, batch_index, slot_count):
    span_count = owners.shape[0]
    span_ids = jnp.arange(span_count, dtype=jnp.int32)
    same_owner = owners[:, None] == owners[None, :]
    earlier = span_ids[None, :] < span_ids[:, None]
    owner_ranks = jnp.sum((same_owner & earlier).astype(jnp.int32), axis=1)
    slot_of = owners * slot_count + owner_ranks
    own_span = owners == batch_index
    slot_ids = jnp.arange(slot_count, dtype=jnp.int32)
    select = ((owner_ranks[None, :] == slot_ids[:, None]) & own_span[None, :]).astype(jnp.float32)
    filled = jnp.sum(select, axis=1, keepdims=True)
    return (slot_of, select, filled)


def scores_of(query, key, same):
    scores = product(query, key, "qhe,khe->hqk") * SCORE_SCALE
    return jnp.where(same[None], scores, MASKED_SCORE)


def layer_forward(rows, trained, blocks, wide, gains, offsets, same):
    scale_q, scale_v, bias_q, bias_v = trained
    rows_low = low(rows)
    total = rows.shape[0]
    projected = sum(
        product(rows_low[:, h * HALF : (h + 1) * HALF], wide[h, 0], "td,rd->tr") for h in range(2)
    )
    u_q, u_v = low(scale_q * projected), low(scale_v * projected)
    adapt_q = jnp.concatenate([product(u_q, wide[h, 1], "tr,rw->tw") for h in range(2)], 1)
    adapt_v = jnp.concatenate([product(u_v, wide[h, 1], "tr,rw->tw") for h in range(2)], 1)
    frozen = [
        jnp.concatenate([product(rows_low, blocks[h, part], "td,dw->tw") for h in range(2)], 1)
        for part in range(3)
    ]
    query = low(frozen[0] + bias_q * adapt_q).reshape(total, -1, HDIM)
    key = low(frozen[1]).reshape(total, -1, HDIM)
    value = low(frozen[2] + bias_v * adapt_v).reshape(total, -1, HDIM)
    chances = jax.nn.softmax(scores_of(query, key, same), axis=-1)
    mixed = low(product(low(chances), value, "hqk,khe->qhe").reshape(total, D))
    first = rows + sum(
        product(mixed[:, h * HALF : (h + 1) * HALF], blocks[h, 3], "tw,dw->td") for h in range(2)
    )
    middle = normalize(first, gains[0], offsets[0])
    middle_low = low(middle)
    before = [
        [product(middle_low, blocks[h, 4 + 2 * j], "td,df->tf") for j in range(4)] for h in range(2)
    ]
    feed = 0.0
    for h in range(2):
        for j in range(4):
            active = low(jax.nn.gelu(before[h][j], approximate=False))
            feed = feed + product(active, blocks[h, 5 + 2 * j], "tf,df->td")
    second = middle + feed
    result = normalize(second, gains[1], offsets[1])
    return result, (projected, adapt_q, adapt_v, query, key, value, first, before, second)


def layer_backward(upstream, kept, trained, blocks, wide, gains, offsets, same):
    scale_q, scale_v, bias_q, bias_v = trained
    projected, adapt_q, adapt_v, query, key, value, first, before, second = kept
    total = first.shape[0]
    second_grad = norm_back(second, gains[1], offsets[1], upstream)
    feed_grad = low(second_grad)
    middle_grad = second_grad
    for h in range(2):
        for j in range(4):
            active_grad = product(feed_grad, blocks[h, 5 + 2 * j], "td,df->tf")
            before_grad = low(gelu_back(before[h][j], active_grad))
            middle_grad = middle_grad + product(before_grad, blocks[h, 4 + 2 * j], "tf,df->td")
    first_grad = norm_back(first, gains[0], offsets[0], middle_grad)
    branch = low(first_grad)
    mixed_grad = jnp.concatenate([product(branch, blocks[h, 3], "td,dw->tw") for h in range(2)], 1)
    mixed_grad = low(mixed_grad).reshape(total, -1, HDIM)
    chances = jax.nn.softmax(scores_of(query, key, same), axis=-1)
    chance_grad = product(mixed_grad, value, "qhe,khe->hqk")
    inner = jnp.sum(chances * chance_grad, axis=-1, keepdims=True)
    score_grad = low(chances * (chance_grad - inner))
    query_grad = low(product(score_grad, key, "hqk,khe->qhe") * SCORE_SCALE).reshape(total, D)
    key_grad = low(product(score_grad, query, "hqk,qhe->khe") * SCORE_SCALE).reshape(total, D)
    value_grad = low(product(low(chances), mixed_grad, "hqk,qhe->khe")).reshape(total, D)
    query_wide, value_wide = query_grad.astype(jnp.float32), value_grad.astype(jnp.float32)
    back_q, back_v = low(bias_q * query_wide), low(bias_v * value_wide)
    sums_q = sums_v = 0.0
    input_grad = first_grad
    from_basis = [0.0, 0.0]
    for h in range(2):
        part = slice(h * HALF, (h + 1) * HALF)
        from_q = product(back_q[:, part], wide[h, 1], "tw,rw->tr")
        from_v = product(back_v[:, part], wide[h, 1], "tw,rw->tr")
        sums_q = sums_q + jnp.sum(projected * from_q, axis=0)
        sums_v = sums_v + jnp.sum(projected * from_v, axis=0)
        projected_grad = low(scale_q * from_q + scale_v * from_v)
        from_basis = [from_basis[k] + jnp.dot(projected_grad, wide[k, 0], preferred_element_type=jnp.float32) for k in range(2)]
        for number, grad in enumerate((query_grad, key_grad, value_grad)):
            input_grad = input_grad + product(grad[:, part], blocks[h, number], "tw,dw->td")
    input_grad = input_grad + jnp.concatenate(from_basis, 1)
    grads = jnp.concatenate(
        [sums_q, sums_v, jnp.sum(query_wide * adapt_q, axis=0), jnp.sum(value_wide * adapt_v, axis=0)]
    )
    return input_grad, grads


def on_device(
    inputs, cotangent, lengths, owners, vectors, first_moment, second_moment,
    weight_in, weight_out, weight_up, weight_down, basis_a, basis_b, norm_gain, norm_bias,
):
    sub = lax.axis_size("batch") // GROUPS
    core = lax.axis_index("tensor")
    batch_index = lax.axis_index("batch")
    slot_count = vectors.shape[0]
    slot_of, select, filled = owner_tables(owners, batch_index, slot_count)
    all_slots = lax.all_gather(vectors, "batch", axis=0, tiled=True)
    flat = jnp.take(all_slots, slot_of, axis=0).reshape(LAYERS, 2 * R + 2 * D)
    trained = [
        (flat[l, :R], flat[l, R : 2 * R], flat[l, 2 * R : 2 * R + D], flat[l, 2 * R + D :])
        for l in range(LAYERS)
    ]
    pack_wide, pack = pack_weights(sub, weight_in, weight_out, weight_up, weight_down, basis_a, basis_b)
    wide, full = gather_weights(sub, pack_wide, pack)
    swap = functools.partial(lax.all_to_all, axis_name="tensor", tiled=True)
    rows = swap(inputs, split_axis=0, concat_axis=1)[0].astype(jnp.float32)
    upstream = swap(cotangent, split_axis=0, concat_axis=1)[0].astype(jnp.float32)
    ids = segment_ids(lax.dynamic_index_in_dim(lengths[:, 0], core, 0, False), rows.shape[0])
    same = ids[:, None] == ids[None, :]
    kept = []
    for l in range(LAYERS):
        rows, saved = layer_forward(
            rows, trained[l], full[:, 12 * l : 12 * (l + 1)], wide, norm_gain[l], norm_bias[l], same
        )
        kept.append(saved)
    grads = [None] * LAYERS
    for l in reversed(range(LAYERS)):
        upstream, grads[l] = layer_backward(
            upstream, kept[l], trained[l], full[:, 12 * l : 12 * (l + 1)], wide, norm_gain[l], norm_bias[l], same
        )
    results = swap(low(rows)[None], split_axis=1, concat_axis=0)
    input_grads = swap(upstream[None], split_axis=1, concat_axis=0)
    full_grad = lax.psum(jnp.concatenate(grads).reshape(slot_of.shape[0], -1), ("batch", "tensor"))
    own_grad = jnp.dot(
        select, full_grad, precision=lax.Precision.HIGHEST, preferred_element_type=jnp.float32
    )
    new_one = (FIRST_BETA * first_moment + (1.0 - FIRST_BETA) * own_grad) * filled
    new_two = (SECOND_BETA * second_moment + (1.0 - SECOND_BETA) * own_grad * own_grad) * filled
    fixed_one = new_one / (1.0 - FIRST_BETA**STEP)
    fixed_two = new_two / (1.0 - SECOND_BETA**STEP)
    updated = (
        vectors
        - LEARN_RATE * (fixed_one / (jnp.sqrt(fixed_two) + ADAM_EPSILON) + WEIGHT_DECAY * vectors)
    ) * filled
    return (results, input_grads, own_grad, new_one, new_two, updated, low(updated))


def solution(mesh):
    rows_spec = P(None, ("batch", "tensor"), None)
    split = P("batch", None)
    return jax.shard_map(
        on_device,
        mesh=mesh,
        in_specs=(
            rows_spec, rows_spec, P(None, "batch", None), P(), split, split, split,
            P(None, "batch", None, "tensor"), P(None, "tensor", "batch"), P(None, "batch", "tensor"),
            P(None, "tensor", "batch"), split, P("tensor", "batch"), P(), P(),
        ),
        out_specs=(rows_spec, rows_spec, split, split, split, split, split),
        check_vma=False,
    )
```

time: 781 us -> 691 us (0.88)
  waiting for transfers between devices: 259 us -> 0.01 us
  matrix products: 190 us -> 352 us
  Pallas kernels: 0 us -> 128 us
  blocking collectives: 169 us -> 79.1 us
  other arithmetic: 69.1 us -> 46.1 us
  between operations: 17.7 us -> 3.07 us
  starting transfers between devices: 1.5 us -> 16 us
    all_gather x5 -> x0, waiting for transfers between devices: 204 us -> none  [the longest x1 78.8 us: on_device(): lax.all_gather(weight_up, 'batch', axis=1, tiled=True)]
    dot_general x68 -> x110, matrix products: 125 us -> 319 us  [product(): return jnp.einsum(form, left, right, preferred_element_type=jnp.float32)]
    pallas_call x0 -> x1, Pallas kernels: none -> 128 us  [gather_weights(): pl.pallas_call(functools.partial(gather_kernel, sub), out_shape=(jax.Shap...]
    all_gather x17 -> x0, blocking collectives: 83.1 us -> none  [the longest x1 43.4 us: on_device(): lax.all_gather(basis_b, 'batch', axis=1, tiled=True)]
    dot_general x16 -> x8, matrix products: 64.4 us -> 10.1 us  [layer_backward(): jnp.dot(projected_grad, wide[k, 0], preferred_element_type=jnp.float32)]
    reduce_scatter x16 -> x0, waiting for transfers between devices: 52.3 us -> none  [the longest x4 17.4 us: layer_forward(): lax.psum_scatter(jnp.dot(active, weight_down, preferred_element_type=jnp....]
    dot_general x0 -> x14, local copies, waits for them, and re-layouts: none -> 29.5 us  [product(): return jnp.einsum(form, left, right, preferred_element_type=jnp.float32)]
    unnamed x450 -> x299, local copies, waits for them, and re-layouts: 47.7 us -> 20.5 us
  transfers between devices with their start and end apart: 21 -> 4, of which waited for: 11 -> 0; matrix products, arithmetic and copies ran while one was open for 20% -> 62% of each run, Pallas kernels for 0% -> 19%
where the time goes in v1:
time: 691 us; the launch traced here: 681 us
  matrix products  352 us (51%)
  Pallas kernels  128 us (19%)
  blocking collectives  79.1 us (11%)
  local copies, waits for them, and re-layouts  57.3 us (8%)
  other arithmetic  46.1 us (7%)
  starting transfers between devices  16 us (2%)
    dot_general x110, matrix products, product(): return jnp.einsum(form, left, right, preferred_element_type=jnp.float32)  319 us
    pallas_call x1, Pallas kernels, gather_weights(): pl.pallas_call(functools.partial(gather_kernel, sub), out_shape=(jax.Shap...  128 us
    all_gather x1, blocking collectives, on_device(): all_slots = lax.all_gather(vectors, 'batch', axis=0, tiled=True)  40.9 us
    psum x1, blocking collectives, on_device(): lax.psum(jnp.concatenate(grads).reshape(slot_of.shape[0], -1), ('batch',...  38.2 us
    dot_general x14, local copies, waits for them, and re-layouts, product(): return jnp.einsum(form, left, right, preferred_element_type=jnp.float32)  29.5 us
    convert_element_type x14, other arithmetic, low(): return values.astype(jnp.bfloat16)  26.1 us
    sub x2, matrix products, layer_forward(): chances = jax.nn.softmax(scores_of(query, key, same), axis=-1)  21.4 us
    unnamed x299, local copies, waits for them, and re-layouts  20.5 us
  transfers between devices with their start and end apart: 4, of which 0 were waited for; matrix products, arithmetic and copies ran while one was open for 62% of the time, Pallas kernels for 19%

profile of v1, /device:TPU:0, one launch (start us, length us, event | category | flops | bytes accessed | tf_op | source)
XLA Modules:
  0.0 680.6 jit_solution(2263853854187434837)
XLA Ops:
  0.7 3.7 all-to-all-start
  7.2 127.5 %shard_map.198 = (bf16[2,2,1024,384]{3,2,1,0:T(8,128)(2,1)}, bf16[2,24,768,384]{3,2,1,0:T(8,128)(2,1)}) custom-call(bf16[2,64,384]{2,1,0:T(8,128)(2,1)} %pad_maximum_fusion.26.pack_wide, bf16[24,48,384]{2,1,0:T(8,128)(2,1)} %copy-done.47), custom_call_target="tpu_custom_call" | custom-call | tf_op jit(solution)/shard_map/pallas_call | solution.py:279
  134.7 2.7 slice_bitcast_fusion.11
  137.4 4.3 all-to-all-start.2
  141.7 3.3 fusion.117
  150.7 40.9 %all_gather.3 = f32[512,28]{1,0:T(8,128)S(1)} all-gather(f32[32,28]{1,0:T(8,128)S(1)} %copy-done.87), channel_id=1, replica_groups=mesh['batch'=16,'tensor'=2] {'batch'}, dimensions={0}, use_global_device_ids=true | all-gather | bytes 60928 | tf_op jit(solution)/shard_map/all_gather | solution.py:458
  197.7 2.6 convolution_add_fusion.1
  200.3 2.9 copy.212
  205.4 2.7 fusion.650
  215.2 2.6 fusion.419
  220.8 10.6 %fusion.803 = (f32[12,512]{1,0:T(8,128)S(1)}, f32[12,512,512]{1,2,0:T(8,128)}) fusion(pred[512,512]{0,1:T(8,128)(4,1)S(1)} %broadcast_compare_fusion, bf16[512,12,64]{0,2,1:T(8,128)(2,1)} %fusion.25, bf16[512,6,64]{0,2,1:T(8,128)(2,1)} %bitcast.775, bf16[512,6,64]{0,2,1:T(8,128)(2,1)} %bitcast.773), kind=kOutput, calls=%fused_computation.1039 | convolution fusion | flops 415629824 | bytes 14442496 | tf_op jit(solution)/shard_map/sub | solution.py:384
  232.9 6.1 fusion.33
  241.6 2.8 fusion.804
  257.1 2.6 slice_bitcast_fusion.9
  259.7 3.4 fusion.379
  267.5 3.6 fusion.355
  271.0 3.3 fusion.343
  274.3 3.3 fusion.331
  277.7 3.3 fusion.319
  281.0 5.0 fusion.805
  323.9 2.7 fusion.27
  326.6 10.7 %fusion.806 = (f32[12,512]{1,0:T(8,128)S(1)}, f32[12,512,512]{1,2,0:T(8,128)}) fusion(pred[512,512]{0,1:T(8,128)(4,1)S(1)} %broadcast_compare_fusion, bf16[512,12,64]{0,2,1:T(8,128)(2,1)} %fusion.27, bf16[512,6,64]{0,2,1:T(8,128)(2,1)} %convolution_convert_fusion.4, bf16[512,6,64]{0,2,1:T(8,128)(2,1)} %convolution_convert_fusion.5), kind=kOutput, calls=%fused_computation.1042 | convolution fusion | flops 415629824 | bytes 14442496 | tf_op jit(solution)/shard_map/sub | solution.py:384
  338.9 6.2 fusion.39
  364.8 3.5 fusion.271
  368.3 3.2 fusion.283
  371.5 3.2 fusion.259
  374.7 3.6 fusion.247
  378.4 3.2 fusion.235
  381.6 3.2 fusion.223
  384.8 3.2 fusion.211
  388.0 3.7 fusion.808
  393.4 3.0 fusion.796
  398.4 6.4 reduce.33
  406.9 4.3 all-to-all-start.1
  412.3 5.5 fusion.288
  417.8 5.5 fusion.276
  423.2 5.5 fusion.264
  428.7 5.5 fusion.252
  434.2 5.9 fusion.240
  440.0 5.5 fusion.228
  445.5 5.5 fusion.216
  451.0 9.1 %multiply_reduce_fusion.12 = (f32[512]{0:T(512)S(1)}, f32[512,768]{1,0:T(8,128)}) fusion(f32[512,768]{1,0:T(8,128)S(1)} %get-tuple-element.100, f32[512]{0:T(512)S(1)} %broadcast_multiply_fusion.1, f32[768]{0:T(1024)S(1)} %get-tuple-element.28, bf16[2,24,768,384]{3,2,1,0:T(8,128)(2,1)} %get-tuple-element.9, f32[512,384]{1,0:T(8,128)} %copy-done.55, ...), kind=kOutput, calls=%fused_computation.92 | convolution fusion | flops 623246848 | bytes 18490368 | tf_op jit(solution)/shard_map/tf,df->td/dot_general | solution.py:335
  465.4 10.4 %multiply_reduce_fusion.1 = (f32[12,512]{1,0:T(8,128)S(1)}, f32[12,512,512]{1,2,0:T(8,128)}) fusion(f32[12,512,512]{1,2,0:T(8,128)} %get-tuple-element.98, f32[12,512]{1,0:T(8,128)S(1)} %get-tuple-element.97, bf16[512,12,64]{0,2,1:T(8,128)(2,1)S(1)} %copy-done.66, bf16[512,6,64]{0,2,1:T(8,128)(2,1)S(1)} %convolution_convert_fusion.2, ...), kind=kOutput, calls=%fused_computation.6 | convolution fusion | flops 412477440 | bytes 26787840 | tf_op jit(solution)/shard_map/qhe,khe->hqk/dot_general | solution.py:335
  477.5 6.9 %multiply_convert_fusion.1 = bf16[12,512,512]{1,2,0:T(8,128)(2,1)S(1)} fusion(f32[12,512,512]{1,2,0:T(8,128)} %get-tuple-element.106, f32[12,512]{1,0:T(8,128)S(1)} %get-tuple-element.105, f32[12,512,512]{1,2,0:T(8,128)S(1)} %bitcast.738, f32[12,512]{1,0:T(8,128)S(1)} %get-tuple-element.97), kind=kLoop, calls=%fused_computation.5 | loop fusion | flops 12582912 | bytes 31506432 | tf_op jit(solution)/shard_map/convert_element_type | solution.py:339
  487.8 3.3 multiply_reduce_fusion.6
  509.2 2.6 multiply_reduce_fusion.11
  514.6 5.7 fusion.396
  520.4 5.5 fusion.384
  525.9 5.5 fusion.372
  531.3 5.5 fusion.360
  536.8 5.5 fusion.348
  542.3 5.9 fusion.336
  548.2 5.5 fusion.324
  553.7 10.1 %multiply_reduce_fusion.10 = (f32[512]{0:T(512)S(1)}, f32[512,768]{1,0:T(8,128)}) fusion(f32[512,768]{1,0:T(8,128)} %copy-done.14, f32[512]{0:T(512)S(1)} %copy-done.99, f32[768]{0:T(1024)S(1)} %copy-done.111, bf16[2,24,768,384]{3,2,1,0:T(8,128)(2,1)} %get-tuple-element.9, f32[512,384]{1,0:T(8,128)} %fusion.315, bf16[512,768]{1,0:T(8,128)(2,1)} %add_convert_fusion.6, ...), kind=kOutput, calls=%fused_computation.85 | convolution fusion | flops 623246848 | bytes 18490368 | tf_op jit(solution)/shard_map/tf,df->td/dot_general | solution.py:335
  563.8 3.5 fusion.793
  576.1 10.3 %multiply_reduce_fusion = (f32[12,512]{1,0:T(8,128)S(1)}, f32[12,512,512]{1,2,0:T(8,128)}) fusion(f32[12,512,512]{1,2,0:T(8,128)} %get-tuple-element.92, f32[12,512]{1,0:T(8,128)S(1)} %copy-done.103, bf16[512,12,64]{0,2,1:T(8,128)(2,1)S(1)} %copy-done.64, bf16[512,6,64]{0,2,1:T(8,128)(2,1)S(1)} %convolution_convert_fusion, ...), kind=kOutput, calls=%fused_computation.4 | convolution fusion | flops 412477440 | bytes 26787840 | tf_op jit(solution)/shard_map/qhe,khe->hqk/dot_general | solution.py:335
  590.3 7.3 %multiply_convert_fusion = bf16[12,512,512]{1,2,0:T(8,128)(2,1)S(1)} fusion(f32[12,512,512]{1,2,0:T(8,128)} %get-tuple-element.112, f32[12,512]{1,0:T(8,128)S(1)} %get-tuple-element.111, f32[12,512,512]{1,2,0:T(8,128)S(1)} %bitcast.736, f32[12,512]{1,0:T(8,128)S(1)} %copy-done.103), kind=kLoop, calls=%fused_computation.3 | loop fusion | flops 12582912 | bytes 31506432 | tf_op jit(solution)/shard_map/convert_element_type | solution.py:339
  603.3 2.8 fusion.414
  606.1 2.9 fusion.410
  609.0 2.8 fusion.407
  611.8 2.8 fusion.404
  622.5 38.2 %psum.7 = f32[256,28]{1,0:T(8,128)S(1)} all-reduce(f32[256,28]{1,0:T(8,128)S(1)} %reshape.342), channel_id=1, replica_groups=mesh['batch'=16,'tensor'=2] {'batch','tensor'}, use_global_device_ids=true, to_apply=%region_37.38 | all-reduce | flops 7168 | bytes 57344 | tf_op jit(solution)/shard_map/psum | solution.py:484
  669.1 2.8 copy.242
  671.9 3.7 all-to-all-start.3
  (470 shorter events, 182.8 us)
Async XLA Ops:
  0.7 136.7 %all-to-all-start = ((bf16[2,256,768]{2,1,0:T(8,128)(2,1)}), bf16[2,256,768]{2,1,0:T(8,128)(2,1)S(1)}, u32[]{:S(2)}, u32[]{:S(2)}) async-start(bf16[2,256,768]{2,1,0:T(8,128)(2,1)} %param.15), calls=%async_computation | async-start | bytes 1572864 | tf_op jit(solution)/shard_map/all_to_all | solution.py:467
  137.4 254.4 %all-to-all-start.2 = ((bf16[2,256,768]{2,1,0:T(8,128)(2,1)}), bf16[2,256,768]{2,1,0:T(8,128)(2,1)}, u32[]{:S(2)}, u32[]{:S(2)}) async-start(bf16[2,256,768]{2,1,0:T(8,128)(2,1)} %param.16), calls=%async_computation.2 | async-start | bytes 1572864 | tf_op jit(solution)/shard_map/all_to_all | solution.py:468
  150.1 42.4 %copy-start.112 = (s32[256]{0:T(256)}, s32[256]{0:T(256)S(1)}, u32[]{:S(2)}) copy-start(s32[256]{0:T(256)S(1)} %convert_reduce_fusion) | copy-start | bytes 3076
  192.8 15.3 %copy-start.77 = (f32[1,1024]{1,0:T(1,128)}, f32[1,1024]{1,0:T(1,128)S(1)}, u32[]{:S(2)}) copy-start(f32[1,1024]{1,0:T(1,128)S(1)} %get-tuple-element.85) | copy-start | bytes 12292
  192.9 18.3 %copy-start.79 = (f32[1,1024]{1,0:T(1,128)}, f32[1,1024]{1,0:T(1,128)S(1)}, u32[]{:S(2)}) copy-start(f32[1,1024]{1,0:T(1,128)S(1)} %get-tuple-element.86) | copy-start | bytes 12292
  192.9 98.2 %copy-start.81 = (f32[1,1024]{1,0:T(1,128)}, f32[1,1024]{1,0:T(1,128)S(1)}, u32[]{:S(2)}) copy-start(f32[1,1024]{1,0:T(1,128)S(1)} %get-tuple-element.84) | copy-start | bytes 12292
  192.9 102.1 %copy-start.83 = (f32[1,1024]{1,0:T(1,128)}, f32[1,1024]{1,0:T(1,128)S(1)}, u32[]{:S(2)}) copy-start(f32[1,1024]{1,0:T(1,128)S(1)} %get-tuple-element.87) | copy-start | bytes 12292
  192.9 24.9 %copy-start.90 = (f32[768]{0:T(1024)}, f32[768]{0:T(1024)S(1)}, u32[]{:S(2)}) copy-start(f32[768]{0:T(1024)S(1)} %get-tuple-element.23) | copy-start | bytes 9220
  192.9 25.5 %copy-start.92 = (f32[768]{0:T(1024)}, f32[768]{0:T(1024)S(1)}, u32[]{:S(2)}) copy-start(f32[768]{0:T(1024)S(1)} %get-tuple-element.24) | copy-start | bytes 9220
  193.0 121.6 %copy-start.96 = (f32[768]{0:T(1024)}, f32[768]{0:T(1024)S(1)}, u32[]{:S(2)}) copy-start(f32[768]{0:T(1024)S(1)} %get-tuple-element.21) | copy-start | bytes 9220
  193.0 130.9 %copy-start.94 = (f32[768]{0:T(1024)}, f32[768]{0:T(1024)S(1)}, u32[]{:S(2)}) copy-start(f32[768]{0:T(1024)S(1)} %get-tuple-element.22) | copy-start | bytes 9220
  200.3 10.9 %copy-start.2 = (f32[1024,512]{0,1:T(8,128)}, f32[1024,512]{0,1:T(8,128)S(1)}, u32[]{:S(2)}) copy-start(f32[1024,512]{0,1:T(8,128)S(1)} %convolution_add_fusion.1) | copy-start | bytes 6291460
  220.8 10.7 %copy-start.32 = (f32[512,6,64]{0,2,1:T(8,128)S(1)}, f32[512,6,64]{0,2,1:T(8,128)}, u32[]{:S(2)}) copy-start(f32[512,6,64]{0,2,1:T(8,128)} %fusion.646) | copy-start | bytes 2359300
  220.8 10.7 %copy-start.34 = (f32[512,6,64]{0,2,1:T(8,128)S(1)}, f32[512,6,64]{0,2,1:T(8,128)}, u32[]{:S(2)}) copy-start(f32[512,6,64]{0,2,1:T(8,128)} %fusion.644) | copy-start | bytes 2359300
  220.8 10.7 %copy-start.43 = (f32[384,512]{1,0:T(8,128)S(1)}, f32[384,512]{1,0:T(8,128)}, u32[]{:S(2)}) copy-start(f32[384,512]{1,0:T(8,128)} %fusion.423) | copy-start | bytes 2359300
  232.9 14.0 %slice-start = ((s8[28311552]{0:T(1024)(128)(4,1)}), s8[4194304]{0:T(1024)(128)(4,1)S(1)}, s32[]{:S(2)}) async-start(s8[28311552]{0:T(1024)(128)(4,1)} %bitcast.733), calls=%async_computation.4 | async-start | bytes 8388608
  232.9 14.0 %slice-start.1 = ((s8[28311552]{0:T(1024)(128)(4,1)}), s8[4194304]{0:T(1024)(128)(4,1)S(1)}, s32[]{:S(2)}) async-start(s8[28311552]{0:T(1024)(128)(4,1)} %bitcast.733), calls=%async_computation.5 | async-start | bytes 8388608
  232.9 14.0 %slice-start.2 = ((s8[28311552]{0:T(1024)(128)(4,1)}), s8[4194304]{0:T(1024)(128)(4,1)S(1)}, s32[]{:S(2)}) async-start(s8[28311552]{0:T(1024)(128)(4,1)} %bitcast.733), calls=%async_computation.6 | async-start | bytes 8388608
  232.9 14.0 %slice-start.3 = ((s8[28311552]{0:T(1024)(128)(4,1)}), s8[4194304]{0:T(1024)(128)(4,1)S(1)}, s32[]{:S(2)}) async-start(s8[28311552]{0:T(1024)(128)(4,1)} %bitcast.733), calls=%async_computation.7 | async-start | bytes 8388608
  232.9 14.0 %slice-start.4 = ((s8[28311552]{0:T(1024)(128)(4,1)}), s8[4194304]{0:T(1024)(128)(4,1)S(1)}, s32[]{:S(2)}) async-start(s8[28311552]{0:T(1024)(128)(4,1)} %bitcast.733), calls=%async_computation.8 | async-start | bytes 8388608
  232.9 14.0 %slice-start.5 = ((s8[28311552]{0:T(1024)(128)(4,1)}), s8[4194304]{0:T(1024)(128)(4,1)S(1)}, s32[]{:S(2)}) async-start(s8[28311552]{0:T(1024)(128)(4,1)} %bitcast.733), calls=%async_computation.9 | async-start | bytes 8388608
  244.4 36.6 %copy-start.14 = (f32[512,768]{1,0:T(8,128)}, f32[512,768]{1,0:T(8,128)S(1)}, u32[]{:S(2)}) copy-start(f32[512,768]{1,0:T(8,128)S(1)} %get-tuple-element.94) | copy-start | bytes 4718596
  244.4 36.5 %copy-start.98 = (f32[512]{0:T(512)}, f32[512]{0:T(512)S(1)}, u32[]{:S(2)}) copy-start(f32[512]{0:T(512)S(1)} %broadcast_multiply_fusion.3) | copy-start | bytes 6148
  246.4 34.6 %copy-start.104 = (f32[512]{0:T(512)}, f32[512]{0:T(512)S(1)}, u32[]{:S(2)}) copy-start(f32[512]{0:T(512)S(1)} %fusion.672) | copy-start | bytes 6148
  246.5 34.5 %copy-start.110 = (f32[768]{0:T(1024)}, f32[768]{0:T(1024)S(1)}, u32[]{:S(2)}) copy-start(f32[768]{0:T(1024)S(1)} %get-tuple-element.27) | copy-start | bytes 9220
  246.5 100.4 %copy-start.85 = (f32[768]{0:T(1024)}, f32[768]{0:T(1024)S(1)}, u32[]{:S(2)}) copy-start(f32[768]{0:T(1024)S(1)} %get-tuple-element.26) | copy-start | bytes 9220
  255.0 19.3 %copy-start.50 = (f32[512,384]{1,0:T(8,128)}, f32[512,384]{1,0:T(8,128)S(1)}, u32[]{:S(2)}) copy-start(f32[512,384]{1,0:T(8,128)S(1)} %fusion.339) | copy-start | bytes 2359300
  255.6 22.0 %copy-start.49 = (f32[512,384]{1,0:T(8,128)}, f32[512,384]{1,0:T(8,128)S(1)}, u32[]{:S(2)}) copy-start(f32[512,384]{1,0:T(8,128)S(1)} %fusion.327) | copy-start | bytes 2359300
  286.0 60.9 %copy-start.8 = (f32[512,768]{1,0:T(8,128)}, f32[512,768]{1,0:T(8,128)S(1)}, u32[]{:S(2)}) copy-start(f32[512,768]{1,0:T(8,128)S(1)} %get-tuple-element.96) | copy-start | bytes 4718596
  286.1 60.8 %copy-start.74 = (f32[512]{0:T(512)}, f32[512]{0:T(512)S(1)}, u32[]{:S(2)}) copy-start(f32[512]{0:T(512)S(1)} %broadcast_multiply_fusion.2) | copy-start | bytes 6148
  286.4 60.5 %copy-start.100 = (f32[512]{0:T(512)}, f32[512]{0:T(512)S(1)}, u32[]{:S(2)}) copy-start(f32[512]{0:T(512)S(1)} %fusion.673) | copy-start | bytes 6148
  291.9 32.0 %copy-start.20 = (f32[512,6,64]{0,2,1:T(8,128)}, f32[512,6,64]{0,2,1:T(8,128)S(1)}, u32[]{:S(2)}) copy-start(f32[512,6,64]{0,2,1:T(8,128)S(1)} %fusion.654) | copy-start | bytes 2359300
  326.6 10.7 %copy-start.36 = (f32[512,6,64]{0,2,1:T(8,128)S(1)}, f32[512,6,64]{0,2,1:T(8,128)}, u32[]{:S(2)}) copy-start(f32[512,6,64]{0,2,1:T(8,128)} %fusion.658) | copy-start | bytes 2359300
  326.6 10.7 %copy-start.38 = (f32[512,6,64]{0,2,1:T(8,128)S(1)}, f32[512,6,64]{0,2,1:T(8,128)}, u32[]{:S(2)}) copy-start(f32[512,6,64]{0,2,1:T(8,128)} %fusion.656) | copy-start | bytes 2359300
  351.2 13.5 %copy-start.60 = (f32[512,384]{1,0:T(8,128)}, f32[512,384]{1,0:T(8,128)S(1)}, u32[]{:S(2)}) copy-start(f32[512,384]{1,0:T(8,128)S(1)} %fusion.279) | copy-start | bytes 2359300
  353.1 15.1 %copy-start.62 = (f32[512,384]{1,0:T(8,128)}, f32[512,384]{1,0:T(8,128)S(1)}, u32[]{:S(2)}) copy-start(f32[512,384]{1,0:T(8,128)S(1)} %fusion.291) | copy-start | bytes 2359300
  355.1 16.4 %copy-start.61 = (f32[512,384]{1,0:T(8,128)}, f32[512,384]{1,0:T(8,128)S(1)}, u32[]{:S(2)}) copy-start(f32[512,384]{1,0:T(8,128)S(1)} %fusion.267) | copy-start | bytes 2359300
  357.0 17.7 %copy-start.59 = (f32[512,384]{1,0:T(8,128)}, f32[512,384]{1,0:T(8,128)S(1)}, u32[]{:S(2)}) copy-start(f32[512,384]{1,0:T(8,128)S(1)} %fusion.255) | copy-start | bytes 2359300
  358.9 19.4 %copy-start.58 = (f32[512,384]{1,0:T(8,128)}, f32[512,384]{1,0:T(8,128)S(1)}, u32[]{:S(2)}) copy-start(f32[512,384]{1,0:T(8,128)S(1)} %fusion.243) | copy-start | bytes 2359300
  360.9 20.7 %copy-start.57 = (f32[512,384]{1,0:T(8,128)}, f32[512,384]{1,0:T(8,128)S(1)}, u32[]{:S(2)}) copy-start(f32[512,384]{1,0:T(8,128)S(1)} %fusion.231) | copy-start | bytes 2359300
  362.8 22.0 %copy-start.56 = (f32[512,384]{1,0:T(8,128)}, f32[512,384]{1,0:T(8,128)S(1)}, u32[]{:S(2)}) copy-start(f32[512,384]{1,0:T(8,128)S(1)} %fusion.219) | copy-start | bytes 2359300
  364.8 23.3 %copy-start.55 = (f32[512,384]{1,0:T(8,128)}, f32[512,384]{1,0:T(8,128)S(1)}, u32[]{:S(2)}) copy-start(f32[512,384]{1,0:T(8,128)S(1)} %fusion.207) | copy-start | bytes 2359300
  406.9 265.0 %all-to-all-start.1 = ((bf16[2,2,98304]{2,1,0:T(2,128)(2,1)}), bf16[2,2,98304]{2,1,0:T(2,128)(2,1)}, u32[]{:S(2)}, u32[]{:S(2)}) async-start(bf16[2,2,98304]{2,1,0:T(2,128)(2,1)} %reshape.377), calls=%async_computation.1 | async-start | bytes 1572864 | tf_op jit(solution)/shard_map/all_to_all | solution.py:482
  464.8 11.1 %slice-start.10 = ((s8[12582912]{0:T(1024)(128)(4,1)}), s8[4194304]{0:T(1024)(128)(4,1)S(1)}, s32[]{:S(2)}) async-start(s8[12582912]{0:T(1024)(128)(4,1)} %bitcast.737), calls=%async_computation.14 | async-start | bytes 8388608
  465.4 10.5 %slice-start.11 = ((s8[12582912]{0:T(1024)(128)(4,1)}), s8[4194304]{0:T(1024)(128)(4,1)S(1)}, s32[]{:S(2)}) async-start(s8[12582912]{0:T(1024)(128)(4,1)} %bitcast.737), calls=%async_computation.15 | async-start | bytes 8388608
  465.4 12.1 %slice-start.12 = ((s8[12582912]{0:T(1024)(128)(4,1)}), s8[4194304]{0:T(1024)(128)(4,1)S(1)}, s32[]{:S(2)}) async-start(s8[12582912]{0:T(1024)(128)(4,1)} %bitcast.737), calls=%async_computation.16 | async-start | bytes 8388608
  477.5 6.9 %copy-start.22 = (f32[512,6,64]{0,2,1:T(8,128)S(1)}, f32[512,6,64]{0,2,1:T(8,128)}, u32[]{:S(2)}) copy-start(f32[512,6,64]{0,2,1:T(8,128)} %fusion.652) | copy-start | bytes 2359300
  477.5 6.9 %copy-start.69 = (bf16[512,6,64]{0,2,1:T(8,128)(2,1)S(1)}, bf16[512,6,64]{0,2,1:T(8,128)(2,1)}, u32[]{:S(2)}) copy-start(bf16[512,6,64]{0,2,1:T(8,128)(2,1)} %convolution_convert_fusion.5) | copy-start | bytes 1179652
  477.5 6.9 %copy-start.70 = (bf16[512,6,64]{0,2,1:T(8,128)(2,1)S(1)}, bf16[512,6,64]{0,2,1:T(8,128)(2,1)}, u32[]{:S(2)}) copy-start(bf16[512,6,64]{0,2,1:T(8,128)(2,1)} %convolution_convert_fusion.4) | copy-start | bytes 1179652
  553.7 10.1 %copy-start.107 = (f32[512]{0:T(512)S(1)}, f32[512]{0:T(512)}, u32[]{:S(2)}) copy-start(f32[512]{0:T(512)} %copy-done.106) | copy-start | bytes 6148
  553.7 10.1 %copy-start.105 = (f32[512]{0:T(512)S(1)}, f32[512]{0:T(512)}, u32[]{:S(2)}) copy-start(f32[512]{0:T(512)} %copy-done.104) | copy-start | bytes 6148
  571.5 14.8 %slice-start.7 = ((s8[12582912]{0:T(1024)(128)(4,1)}), s8[4194304]{0:T(1024)(128)(4,1)S(1)}, s32[]{:S(2)}) async-start(s8[12582912]{0:T(1024)(128)(4,1)} %bitcast.735), calls=%async_computation.11 | async-start | bytes 8388608
  576.0 10.3 %slice-start.8 = ((s8[12582912]{0:T(1024)(128)(4,1)}), s8[4194304]{0:T(1024)(128)(4,1)S(1)}, s32[]{:S(2)}) async-start(s8[12582912]{0:T(1024)(128)(4,1)} %bitcast.735), calls=%async_computation.12 | async-start | bytes 8388608
  576.1 11.4 %slice-start.9 = ((s8[12582912]{0:T(1024)(128)(4,1)}), s8[4194304]{0:T(1024)(128)(4,1)S(1)}, s32[]{:S(2)}) async-start(s8[12582912]{0:T(1024)(128)(4,1)} %bitcast.735), calls=%async_computation.13 | async-start | bytes 8388608
  576.1 11.5 %copy-start.33 = (f32[512,6,64]{0,2,1:T(8,128)S(1)}, f32[512,6,64]{0,2,1:T(8,128)}, u32[]{:S(2)}) copy-start(f32[512,6,64]{0,2,1:T(8,128)} %fusion.646) | copy-start | bytes 2359300
  576.1 11.8 %copy-start.35 = (f32[512,6,64]{0,2,1:T(8,128)S(1)}, f32[512,6,64]{0,2,1:T(8,128)}, u32[]{:S(2)}) copy-start(f32[512,6,64]{0,2,1:T(8,128)} %fusion.644) | copy-start | bytes 2359300
  590.3 8.7 %copy-start.40 = (bf16[12,64,512]{2,1,0:T(8,128)(2,1)}, bf16[12,64,512]{2,1,0:T(8,128)(2,1)S(1)}, u32[]{:S(2)}) copy-start(bf16[12,64,512]{2,1,0:T(8,128)(2,1)S(1)} %get-tuple-element.116) | copy-start | bytes 2359300
  590.3 7.4 %copy-start.17 = (f32[512,6,64]{0,2,1:T(8,128)S(1)}, f32[512,6,64]{0,2,1:T(8,128)}, u32[]{:S(2)}) copy-start(f32[512,6,64]{0,2,1:T(8,128)} %fusion.650) | copy-start | bytes 2359300
  590.3 7.4 %copy-start.19 = (f32[512,6,64]{0,2,1:T(8,128)S(1)}, f32[512,6,64]{0,2,1:T(8,128)}, u32[]{:S(2)}) copy-start(f32[512,6,64]{0,2,1:T(8,128)} %fusion.648) | copy-start | bytes 2359300
  590.3 7.4 %copy-start.67 = (bf16[384,512]{1,0:T(8,128)(2,1)S(1)}, bf16[384,512]{1,0:T(8,128)(2,1)}, u32[]{:S(2)}) copy-start(bf16[384,512]{1,0:T(8,128)(2,1)} %convolution_convert_fusion.7) | copy-start | bytes 1179652
  590.3 7.4 %copy-start.68 = (bf16[384,512]{1,0:T(8,128)(2,1)S(1)}, bf16[384,512]{1,0:T(8,128)(2,1)}, u32[]{:S(2)}) copy-start(bf16[384,512]{1,0:T(8,128)(2,1)} %convolution_convert_fusion.6) | copy-start | bytes 1179652
  620.4 40.3 %copy-start.113 = (s32[256]{0:T(256)S(1)}, s32[256]{0:T(256)}, u32[]{:S(2)}) copy-start(s32[256]{0:T(256)} %copy-done.112) | copy-start | bytes 3076
  620.4 40.3 %copy-start.119 = (pred[256]{0:T(512)(128)(4,1)S(1)}, pred[256]{0:T(512)(128)(4,1)}, u32[]{:S(2)}) copy-start(pred[256]{0:T(512)(128)(4,1)} %get-tuple-element.90) | copy-start | bytes 772
  671.9 7.2 %all-to-all-start.3 = ((f32[1,512,768]{2,0,1:T(1,128)}), f32[1,512,768]{2,0,1:T(1,128)S(1)}, u32[]{:S(2)}, u32[]{:S(2)}) async-start(f32[1,512,768]{2,0,1:T(1,128)} %copy.242), calls=%async_computation.3 | async-start | bytes 3145728 | tf_op jit(solution)/shard_map/all_to_all | solution.py:483
  (74 other events, 203.4 us)
